TPU v7x, 256 devices: a whole 4x4x8 slice. The times are simulated.
256 devices in a mesh: text: 16 (over y_hi, x, core), image: 16 (over y_lo, z).
Axes of the slice: x: 4, y: 4 (y_hi: 2, y_lo: 2; y = y_hi * 2 + y_lo), z: 8, core: 2. Of those that a mesh axis runs over, the one named last changes fastest.
Arguments:
- queries: bfloat16 [2048, 4096], P('text'), may hold values from -24 to 24
- keys: bfloat16 [10240, 512], P('image'), may hold values from -24 to 24
- values: bfloat16 [10240, 512], P('image'), may hold values from -6 to 6
- grad_out: bfloat16 [2048, 4096], P('text'), may hold values from -600 to 600
- keep_blocks: int32 [32, 80], P('text', 'image'), may hold values from 0 to 1, as said below
Outputs:
- grad_queries: bfloat16 [2048, 4096], P('text', 'image')
- grad_keys: bfloat16 [10240, 512], P(('image', 'text'))
- grad_values: bfloat16 [10240, 512], P(('image', 'text'))
Inputs may be any that keep to these rules, and one draw needn't show every extreme that they name: `keep_blocks`: the last frame block is kept for every text block.
All inputs are finite; a program needn't handle non-finite values.
Results may differ from a plain program's by a relative error of at most 0.0059.
Values sent between devices are 32-bit elements; how exact they have to be, the bound alone decides.
No kernel may reach another device: no remote copies, remote signals or barrier semaphores. Data moves between devices by JAX's collectives and lax.ppermute only.
A program may use at most 128 MiB of HBM per device.

v0:
```python
import jax
import jax.numpy as jnp
from jax import lax
from jax.sharding import PartitionSpec as P

HD = 128
TBLK = 64
FBLK = 128


floor_score = -1e30


def merged(part, axis, combine):
    gathered = jax.tree.map(lambda a: lax.all_gather(a, axis), part)

    def take(source):
        return jax.tree.map(lambda a: lax.dynamic_index_in_dim(a, source, 0, False), gathered)

    return lax.fori_loop(
        1, lax.axis_size(axis), lambda source, state: combine(state, take(source)), take(0)
    )


def expand_mask(keep_blocks):
    widened = jnp.repeat(jnp.repeat(keep_blocks, TBLK, axis=0), FBLK, axis=1)
    return widened > 0


def query_heads(array, group_index, per_group):
    width = per_group * HD
    piece = array[:, group_index * width : (group_index + 1) * width]
    return piece.reshape(piece.shape[0], per_group, HD)


def key_head(array, group_index):
    return array[:, group_index * HD : (group_index + 1) * HD]


def group_scores(query_group, key_group, kept_mask):
    raw = jnp.einsum(
        "thd,kd->htk", query_group, key_group, preferred_element_type=jnp.float32
    ) * HD ** (-0.5)
    return jnp.where(kept_mask[None], raw, floor_score)


def value_products(grad_group, value_group):
    return jnp.einsum("thd,kd->htk", grad_group, value_group, preferred_element_type=jnp.float32)


def merge_pair(first, second):
    largest = jnp.maximum(first[0], second[0])
    return (
        largest,
        first[1] * jnp.exp(first[0] - largest) + second[1] * jnp.exp(second[0] - largest),
    )


def backward_group(query_group, grad_group, key_group, value_group, kept_mask, log_total, delta):
    scores = group_scores(query_group, key_group, kept_mask)
    probs = jnp.where(kept_mask[None], jnp.exp(scores - log_total[:, :, None]), 0.0)
    grad_probs = value_products(grad_group, value_group)
    grad_scores = probs * (grad_probs - delta[:, :, None])
    return (probs.astype(jnp.bfloat16), grad_scores.astype(jnp.bfloat16))


def on_device(queries, keys, values, grad_out, keep_blocks):
    kept_mask = expand_mask(keep_blocks)
    groups = keys.shape[1] // HD
    per_group = queries.shape[1] // keys.shape[1]
    score_scale = HD ** (-0.5)
    maxima = []
    totals = []
    for group_index in range(groups):
        query_group = query_heads(queries, group_index, per_group)
        key_group = key_head(keys, group_index)
        scores = group_scores(query_group, key_group, kept_mask)
        row_max = jnp.max(scores, axis=2)
        weights = jnp.where(kept_mask[None], jnp.exp(scores - row_max[:, :, None]), 0.0)
        maxima.append(row_max)
        totals.append(jnp.sum(weights, axis=2))
    local_max = jnp.concatenate(maxima, axis=0)
    local_total = jnp.concatenate(totals, axis=0)
    row_max, row_total = merged((local_max, local_total), "image", merge_pair)
    log_total = row_max + jnp.log(row_total)
    partial_delta = []
    for group_index in range(groups):
        query_group = query_heads(queries, group_index, per_group)
        grad_group = query_heads(grad_out, group_index, per_group)
        scores = group_scores(query_group, key_head(keys, group_index), kept_mask)
        head_rows = log_total[group_index * per_group : (group_index + 1) * per_group]
        probs = jnp.where(kept_mask[None], jnp.exp(scores - head_rows[:, :, None]), 0.0)
        grad_probs = value_products(grad_group, key_head(values, group_index))
        partial_delta.append(jnp.sum(probs * grad_probs, axis=2))
    delta = lax.psum(jnp.concatenate(partial_delta, axis=0), "image")
    query_terms = []
    key_terms = []
    value_terms = []
    for group_index in range(groups):
        query_group = query_heads(queries, group_index, per_group)
        grad_group = query_heads(grad_out, group_index, per_group)
        key_group = key_head(keys, group_index)
        head_slice = slice(group_index * per_group, (group_index + 1) * per_group)
        probs_low, grad_scores = backward_group(
            query_group,
            grad_group,
            key_group,
            key_head(values, group_index),
            kept_mask,
            log_total[head_slice],
            delta[head_slice],
        )
        grad_query = (
            jnp.einsum("htk,kd->thd", grad_scores, key_group, preferred_element_type=jnp.float32)
            * score_scale
        )
        query_terms.append(grad_query.reshape(grad_query.shape[0], per_group * HD))
        key_terms.append(
            jnp.einsum("htk,thd->kd", grad_scores, query_group, preferred_element_type=jnp.float32)
            * score_scale
        )
        value_terms.append(
            jnp.einsum("htk,thd->kd", probs_low, grad_group, preferred_element_type=jnp.float32)
        )
    grad_queries = lax.psum_scatter(
        jnp.concatenate(query_terms, axis=1), "image", scatter_dimension=1, tiled=True
    ).astype(jnp.bfloat16)
    grad_keys, grad_values = (
        lax.psum_scatter(
            jnp.concatenate(key_terms, axis=1), "text", scatter_dimension=0, tiled=True
        ),
        lax.psum_scatter(
            jnp.concatenate(value_terms, axis=1), "text", scatter_dimension=0, tiled=True
        ),
    )
    return (grad_queries, grad_keys.astype(jnp.bfloat16), grad_values.astype(jnp.bfloat16))


def solution(mesh):
    return jax.shard_map(
        on_device,
        mesh=mesh,
        in_specs=(
            P("text", None),
            P("image", None),
            P("image", None),
            P("text", None),
            P("text", "image"),
        ),
        out_specs=(P("text", "image"), P(("image", "text"), None), P(("image", "text"), None)),
        check_vma=False,
    )
```

profile of v0, /device:TPU:8, one launch (start us, length us, event | category | flops | bytes accessed | tf_op | source)
XLA Modules:
  0.0 354.3 jit_solution(10918651652179263572)
XLA Ops:
  14.4 1.5 fusion.54
  15.9 1.4 fusion.51
  18.0 2.0 select_reduce_fusion.3
  20.0 1.9 select_reduce_fusion.2
  21.9 36.7 %all-gather.1 = f32[512,128]{1,0:T(8,128)S(1)} all-gather(f32[32,128]{1,0:T(8,128)S(1)} %pad_maximum_fusion.4), channel_id=3, replica_groups=mesh['text'=16,'image'=16] {'image'}, dimensions={0}, use_global_device_ids=true | all-gather | bytes 278528 | tf_op jit(solution)/shard_map/all_gather | solution.py:15
  58.6 30.9 %all-gather = f32[512,128]{1,0:T(8,128)S(1)} all-gather(f32[32,128]{1,0:T(8,128)S(1)} %pad_maximum_fusion.3), channel_id=2, replica_groups=mesh['text'=16,'image'=16] {'image'}, dimensions={0}, use_global_device_ids=true | all-gather | bytes 278528 | tf_op jit(solution)/shard_map/all_gather | solution.py:15
  90.2 11.7 %while.17 = (s32[]{:T(128)}, f32[32,128]{1,0:T(8,128)S(1)}, f32[32,128]{1,0:T(8,128)S(1)}, f32[16,32,128]{2,1,0:T(8,128)}, f32[16,32,128]{2,1,0:T(8,128)}, /*index=5*/s32[]{:T(128)}, s32[]{:T(128)}, s32[]{:T(128)}) while((s32[]{:T(128)}, f32[32,128]{1,0:T(8,128)S(1)}, f32[32,128]{1,0:T(8,128)S(1)}, f32[16,32,128]{2,1,0:T(8,128)}, ...), condition=%wide.region_9.10_spmd, body=%wide.region_8.9_spmd.sunk | while | flops 24581 | bytes 98427 | solution.py:20
  101.9 2.6 fusion.35
  110.0 2.8 copy.147
  113.1 1.7 fusion.42
  114.8 2.1 fusion.46
  117.8 1.7 copy-done.11
  119.5 4.3 %fusion.11 = (f32[8,128]{1,0:T(8,128)S(1)}, f32[8,128]{1,0:T(8,128)S(1)}, f32[8,128]{1,0:T(8,128)S(1)}, f32[8,128]{1,0:T(8,128)S(1)}, f32[640,128,8]{1,0,2:T(8,128)}) fusion(f32[8,128]{1,0:T(8,128)S(1)} %get-tuple-element.189, f32[640,128,8]{1,0,2:T(8,128)S(1)} %copy-done.14, pred[128,640]{0,1:T(8,128)(4,1)S(1)} %bitcast.244, ...), kind=kOutput, calls=%fused_computation.22 | convolution fusion | flops 183496704 | bytes 21512192 | tf_op jit(solution)/shard_map/thd,kd->htk/dot_general | solution.py:48
  123.8 61.9 %psum.7 = f32[32,128]{1,0:T(8,128)S(1)} all-reduce(f32[32,128]{1,0:T(8,128)S(1)} %pad_maximum_fusion.5), channel_id=1, replica_groups=mesh['text'=16,'image'=16] {'image'}, use_global_device_ids=true, to_apply=%region_14.15 | all-reduce | flops 4096 | bytes 32768 | tf_op jit(solution)/shard_map/psum | solution.py:95
  185.7 8.2 %fusion.13 = (bf16[8,128,640]{1,2,0:T(8,128)(2,1)S(1)}, bf16[8,128,640]{1,2,0:T(8,128)(2,1)S(1)}, bf16[8,128,640]{1,2,0:T(8,128)(2,1)S(1)}, bf16[8,128,640]{1,2,0:T(8,128)(2,1)S(1)}) fusion(f32[640,128,8]{1,0,2:T(8,128)} %get-tuple-element.193, f32[8,128]{1,0:T(8,128)S(1)} %get-tuple-element.182, f32[8,128]{1,0:T(8,128)S(1)} %get-tuple-element.189, ...), kind=kLoop, calls=%fused_computation.24 | loop fusion | flops 18350080 | bytes 26329088 | tf_op jit(solution)/shard_map/convert_element_type | solution.py:64
  196.9 1.5 copy.145
  198.4 1.4 convolution_multiply_fusion.3
  200.9 1.8 convolution_multiply_fusion.2
  203.7 1.3 convolution_multiply_fusion
  206.1 1.4 convolution_multiply_fusion.1
  207.7 2.6 pad_maximum_fusion
  212.1 58.2 %reduce-scatter.10.cloned.1.call-done = f32[40,512]{1,0:T(8,128)} async-done(((f32[640,512]{1,0:T(8,128)}), f32[40,512]{1,0:T(8,128)}) %reduce-scatter.10.cloned.1.call-update) | async-done | bytes 81936
  272.0 74.2 %reduce-scatter.8.cloned.1.call-done = f32[128,256]{1,0:T(8,128)} async-done(((f32[128,4096]{1,0:T(8,128)}), f32[128,256]{1,0:T(8,128)}) %reduce-scatter.8.cloned.1.call-update) | async-done | bytes 131088 | tf_op jit(solution)/shard_map/reduce_scatter | solution.py:125
  346.2 1.5 convert_element_type.37
  (127 shorter events, 36.1 us)
Async XLA Ops:
  7.2 3.8 %copy-start.24 = (bf16[128,4096]{1,0:T(8,128)(2,1)S(1)}, bf16[128,4096]{1,0:T(8,128)(2,1)}, u32[]{:S(2)}) copy-start(bf16[128,4096]{1,0:T(8,128)(2,1)} %param.10) | copy-start | bytes 3145732
  7.2 203.2 %reduce-scatter.12.cloned.1.call-start = ((), (), s32[]{:S(2)}) async-start(), calls=%async_computation.5 | async-start | bytes 1392640
  14.4 3.0 copy-start.20
  15.9 2.1 copy-start.25
  17.3 2.6 copy-start
  17.9 2.0 copy-start.12
  58.6 30.9 %copy-start.27 = (f32[512,128]{1,0:T(8,128)}, f32[512,128]{1,0:T(8,128)S(1)}, u32[]{:S(2)}) copy-start(f32[512,128]{1,0:T(8,128)S(1)} %all-gather.1) | copy-start | bytes 786436
  101.9 2.6 copy-start.21
  112.9 157.4 %reduce-scatter.10.cloned.1.call-start = ((), (), s32[]{:S(2)}) async-start(), calls=%async_computation.4 | async-start | bytes 1392640
  113.1 3.9 %copy-start.22 = (bf16[128,1024]{0,1:T(8,128)(2,1)S(1)}, bf16[128,1024]{0,1:T(8,128)(2,1)}, u32[]{:S(2)}) copy-start(bf16[128,1024]{0,1:T(8,128)(2,1)} %copy.155) | copy-start | bytes 786436
  113.1 3.9 %copy-start.29 = (bf16[640,512]{1,0:T(8,128)(2,1)S(1)}, bf16[640,512]{1,0:T(8,128)(2,1)}, u32[]{:S(2)}) copy-start(bf16[640,512]{1,0:T(8,128)(2,1)} %param.9) | copy-start | bytes 1966084
  113.1 4.4 %copy-start.14 = (f32[640,128,8]{1,0,2:T(8,128)S(1)}, f32[640,128,8]{1,0,2:T(8,128)}, u32[]{:S(2)}) copy-start(f32[640,128,8]{1,0,2:T(8,128)} %copy-done.12) | copy-start | bytes 7864324
  114.8 2.7 copy-start.15
  114.8 3.0 copy-start.1
  114.8 4.7 %copy-start.11 = (f32[640,128,8]{1,0,2:T(8,128)S(1)}, f32[640,128,8]{1,0,2:T(8,128)}, u32[]{:S(2)}) copy-start(f32[640,128,8]{1,0,2:T(8,128)} %copy-done.9) | copy-start | bytes 7864324
  114.8 4.7 %copy-start.31 = (bf16[128,1024]{0,1:T(8,128)(2,1)S(1)}, bf16[128,1024]{0,1:T(8,128)(2,1)}, u32[]{:S(2)}) copy-start(bf16[128,1024]{0,1:T(8,128)(2,1)} %copy.153) | copy-start | bytes 786436
  117.0 6.8 %copy-start.16 = (f32[640,128,8]{1,0,2:T(8,128)}, f32[640,128,8]{1,0,2:T(8,128)S(1)}, u32[]{:S(2)}) copy-start(f32[640,128,8]{1,0,2:T(8,128)S(1)} %fusion.46) | copy-start | bytes 7864324
  119.5 4.3 %copy-start.17 = (f32[640,128,8]{1,0,2:T(8,128)}, f32[640,128,8]{1,0,2:T(8,128)S(1)}, u32[]{:S(2)}) copy-start(f32[640,128,8]{1,0,2:T(8,128)S(1)} %fusion.44) | copy-start | bytes 7864324
  185.7 8.8 %copy-start.26 = (bf16[128,1024]{0,1:T(8,128)(2,1)S(1)}, bf16[128,1024]{0,1:T(8,128)(2,1)}, u32[]{:S(2)}) copy-start(bf16[128,1024]{0,1:T(8,128)(2,1)} %copy.150) | copy-start | bytes 786436
  193.9 2.3 copy-start.2
  198.3 5.4 %copy-start.5 = (bf16[8,128,640]{1,2,0:T(8,128)(2,1)S(1)}, bf16[8,128,640]{1,2,0:T(8,128)(2,1)}, u32[]{:S(2)}) copy-start(bf16[8,128,640]{1,2,0:T(8,128)(2,1)} %copy-done.4) | copy-start | bytes 3932164
  198.4 147.8 %reduce-scatter.8.cloned.1.call-start = ((), (), s32[]{:S(2)}) async-start(), calls=%async_computation.3 | async-start | bytes 2228224 | tf_op jit(solution)/shard_map/reduce_scatter | solution.py:125
  200.9 5.2 %copy-start.3 = (bf16[8,128,640]{1,2,0:T(8,128)(2,1)S(1)}, bf16[8,128,640]{1,2,0:T(8,128)(2,1)}, u32[]{:S(2)}) copy-start(bf16[8,128,640]{1,2,0:T(8,128)(2,1)} %copy-done.2) | copy-start | bytes 3932164
  205.1 2.6 copy-start.18
  (11 other events, 18.1 us)
Sparse Core Ops, SparseCore 0:
  113.0 73.2 reduce-scatter.11
  198.5 71.7 reduce-scatter.9
  272.8 73.3 reduce-scatter.7
where the time goes:
time: 358 us; the launch traced here: 354 us
  waiting for transfers between devices  132 us (37%)
  blocking collectives  129 us (36%)
  other arithmetic  27.7 us (8%)
  matrix products  27.1 us (8%)
  local copies, waits for them, and re-layouts  22.7 us (6%)
  between operations  14.3 us (4%)
    reduce_scatter x1, waiting for transfers between devices, on_device(): lax.psum_scatter(jnp.concatenate(query_terms, axis=1), 'image', scatter_d...  74.2 us
    all_gather x2, blocking collectives, merged(): gathered = jax.tree.map(lambda a: lax.all_gather(a, axis), part)  67.6 us
    psum x1, blocking collectives, on_device(): delta = lax.psum(jnp.concatenate(partial_delta, axis=0), 'image')  61.9 us
    unnamed x5, waiting for transfers between devices  58.2 us
    unnamed x78, local copies, waits for them, and re-layouts  17.7 us
    add x15, other arithmetic, merge_pair(): first[1] * jnp.exp(first[0] - largest)  11.4 us
    dot_general x4, matrix products, value_products(): jnp.einsum('thd,kd->htk', grad_group, value_group, preferred_element_type...  8.54 us
    convert_element_type x1, other arithmetic, backward_group(): return (probs.astype(jnp.bfloat16), grad_scores.astype(jnp.bfloat16))  8.2 us
  transfers between devices with their start and end apart: 3, of which 2 were waited for; matrix products, arithmetic and copies ran while one was open for 10% of the time, Pallas kernels for 0%

commit v1 on v0

v1 whole, which is shorter than its diff:
```python
import jax
import jax.numpy as jnp
from jax import lax
from jax.experimental import pallas as pl
from jax.experimental.pallas import tpu as pltpu
from jax.sharding import PartitionSpec as P

HD = 128
TBLK = 64
FBLK = 128
SCALE = HD ** (-0.5)
EXP2_SCALE = SCALE * 1.4426950408889634
MASKED = -1e30
NO_KEY = -1e29
LIMIT = 56 * 1024 * 1024

F32 = jnp.float32
BF16 = jnp.bfloat16


def head(array, index):
    return array[:, index * HD : (index + 1) * HD]


def row_fold(block, combine):
    parts = [block[8 * i : 8 * i + 8] for i in range(block.shape[0] // 8)]
    while len(parts) > 1:
        parts = [combine(parts[i], parts[i + 1]) for i in range(0, len(parts) - 1, 2)] + (
            [parts[-1]] if len(parts) % 2 else []
        )
    return parts[0]


def local_kernel(
    keep_ref, q_ref, do_ref, k_ref, v_ref,
    e_ref, es_ref, at_ref, bt_ref, stat_ref, max_ref,
    s_scr, g_scr,
):
    group = pl.program_id(0)
    heads = q_ref.shape[1] // HD
    rows = q_ref.shape[0]
    blocks = k_ref.shape[0] // FBLK
    copies, stat_rows = stat_ref.shape[0], stat_ref.shape[1] // 2
    first_half = lax.broadcasted_iota(jnp.int32, (1, rows), 1) < TBLK
    bias = [
        jnp.where(
            first_half,
            jnp.where(keep_ref[0, b] > 0, 0.0, MASKED),
            jnp.where(keep_ref[1, b] > 0, 0.0, MASKED),
        ).astype(F32)
        for b in range(blocks)
    ]
    keys = k_ref[...]
    values = v_ref[...]
    maxima, logs, deltas = [], [], []
    for pair in range(heads // 2):
        two = (2 * pair, 2 * pair + 1)
        columns = slice(2 * pair * rows, (2 * pair + 2) * rows)
        q_two = jnp.concatenate([head(q_ref, h) for h in two], axis=0)
        do_two = jnp.concatenate([head(do_ref, h) for h in two], axis=0)
        contract_last = (((1,), (1,)), ((), ()))
        s_scr[:, columns] = lax.dot_general(keys, q_two, contract_last, preferred_element_type=F32)
        g_scr[:, columns] = lax.dot_general(values, do_two, contract_last, preferred_element_type=F32)
        for h in two:
            lanes = slice(h * rows, (h + 1) * rows)
            top = None
            for b in range(blocks):
                block_rows = slice(b * FBLK, (b + 1) * FBLK)
                part = row_fold(s_scr[block_rows, lanes], jnp.maximum) + bias[b]
                top = part if top is None else jnp.maximum(top, part)
            row_max = jnp.maximum(jnp.max(top, axis=0, keepdims=True), NO_KEY)
            total = jnp.zeros((8, rows), F32)
            product = jnp.zeros((8, rows), F32)
            for b in range(blocks):
                block_rows = slice(b * FBLK, (b + 1) * FBLK)
                weight = jnp.exp2((s_scr[block_rows, lanes] + (bias[b] - row_max)) * EXP2_SCALE)
                s_scr[block_rows, lanes] = weight
                total = total + row_fold(weight, jnp.add)
                product = product + row_fold(weight * g_scr[block_rows, lanes], jnp.add)
            total = jnp.sum(total, axis=0, keepdims=True)
            product = jnp.sum(product, axis=0, keepdims=True)
            some = total > 0.0
            safe = jnp.where(some, total, 1.0)
            delta = product / safe
            for b in range(blocks):
                block_rows = slice(b * FBLK, (b + 1) * FBLK)
                weight = s_scr[block_rows, lanes]
                e_ref[block_rows, lanes] = weight.astype(BF16)
                es_ref[block_rows, lanes] = (weight * (g_scr[block_rows, lanes] - delta)).astype(BF16)
            scaled_max = row_max * SCALE
            maxima.append(scaled_max)
            logs.append(jnp.where(some, scaled_max + jnp.log(safe), MASKED))
            deltas.append(delta)
        contract_first = (((0,), (0,)), ((), ()))
        at_ref[:, columns] = lax.dot_general(
            keys, es_ref[:, columns], contract_first, preferred_element_type=F32
        )
        bt_ref[:, columns] = lax.dot_general(
            keys, e_ref[:, columns], contract_first, preferred_element_type=F32
        )
    log_rows = jnp.concatenate(logs, axis=0)
    delta_rows = jnp.concatenate(deltas, axis=0)
    at = pl.multiple_of(group * heads, 8)
    for copy in range(copies):
        stat_ref[copy, pl.ds(at, heads), :] = log_rows
        stat_ref[copy, pl.ds(at + stat_rows, heads), :] = delta_rows
    max_ref[pl.ds(at, heads), :] = jnp.concatenate(maxima, axis=0)


def local_part(keep_blocks, queries, grad_out, keys, values, copies):
    rows, width = queries.shape
    image_rows, key_width = keys.shape
    groups = key_width // HD
    per_group = width // groups
    heads = width // HD
    wide = groups * (per_group // HD) * rows
    wide_block = wide // groups
    flops = 8 * heads * rows * image_rows * HD
    return pl.pallas_call(
        local_kernel,
        grid=(groups,),
        in_specs=[
            pl.BlockSpec(memory_space=pltpu.SMEM),
            pl.BlockSpec((rows, per_group), lambda g: (0, g)),
            pl.BlockSpec((rows, per_group), lambda g: (0, g)),
            pl.BlockSpec((image_rows, HD), lambda g: (0, g)),
            pl.BlockSpec((image_rows, HD), lambda g: (0, g)),
        ],
        out_specs=[
            pl.BlockSpec((image_rows, wide_block), lambda g: (0, g)),
            pl.BlockSpec((image_rows, wide_block), lambda g: (0, g)),
            pl.BlockSpec((HD, wide_block), lambda g: (0, g)),
            pl.BlockSpec((HD, wide_block), lambda g: (0, g)),
            pl.BlockSpec((copies, 2 * heads, rows), lambda g: (0, 0, 0)),
            pl.BlockSpec((heads, rows), lambda g: (0, 0)),
        ],
        out_shape=[
            jax.ShapeDtypeStruct((image_rows, wide), BF16),
            jax.ShapeDtypeStruct((image_rows, wide), BF16),
            jax.ShapeDtypeStruct((HD, wide), F32),
            jax.ShapeDtypeStruct((HD, wide), F32),
            jax.ShapeDtypeStruct((copies, 2 * heads, rows), F32),
            jax.ShapeDtypeStruct((heads, rows), F32),
        ],
        scratch_shapes=[
            pltpu.VMEM((image_rows, wide_block), F32),
            pltpu.VMEM((image_rows, wide_block), F32),
        ],
        compiler_params=pltpu.CompilerParams(vmem_limit_bytes=LIMIT),
        cost_estimate=pl.CostEstimate(
            flops=flops, bytes_accessed=18 * 2**20, transcendentals=heads * rows * image_rows
        ),
        name="local_products",
    )(keep_blocks, queries, grad_out, keys, values)


def query_kernel(all_ref, own_ref, max_ref, at_ref, bt_ref, out_ref, factor_ref, w_scr, d_scr):
    group = pl.program_id(0)
    sources, double, rows = all_ref.shape
    heads = double // 2

    @pl.when(group == 0)
    def _():
        logs = [all_ref[s, 0:heads, :] for s in range(sources)]
        top = logs[0]
        for log in logs[1:]:
            top = jnp.maximum(top, log)
        total = jnp.zeros((heads, rows), F32)
        product = jnp.zeros((heads, rows), F32)
        for s in range(sources):
            share = jnp.exp(logs[s] - top)
            total = total + share
            product = product + share * all_ref[s, heads:double, :]
        w = jnp.exp(max_ref[...] - (top + jnp.log(total)))
        w_scr[...] = w
        d_scr[...] = w * (own_ref[0, heads:double, :] - product / total)

    per_group = at_ref.shape[1] // rows
    at = pl.ds(pl.multiple_of(group * per_group, 8), per_group)
    w_rows = w_scr[at, :]
    d_rows = d_scr[at, :]
    fill = jnp.zeros((rows - 2 * per_group, rows), F32)
    factor_ref[0] = jnp.transpose(jnp.concatenate([w_rows, d_rows, fill], axis=0))
    for h in range(per_group):
        lanes = slice(h * rows, (h + 1) * rows)
        term = (w_rows[h : h + 1] * at_ref[:, lanes] + d_rows[h : h + 1] * bt_ref[:, lanes]) * SCALE
        out_ref[h // 2, 0, :, (h % 2) * HD : (h % 2 + 1) * HD] = jnp.transpose(term)


def query_part(stats, own, maxima, at, bt, z_size, y_size):
    sources, double, rows = stats.shape
    wide = at.shape[1]
    heads = wide // rows
    per_group = 8
    groups = heads // per_group
    per_y = groups // y_size
    pieces = per_group // 2
    return pl.pallas_call(
        query_kernel,
        grid=(groups,),
        in_specs=[
            pl.BlockSpec((sources, double, rows), lambda g: (0, 0, 0)),
            pl.BlockSpec((1, double, rows), lambda g: (0, 0, 0)),
            pl.BlockSpec((heads, rows), lambda g: (0, 0)),
            pl.BlockSpec((HD, per_group * rows), lambda g: (0, g)),
            pl.BlockSpec((HD, per_group * rows), lambda g: (0, g)),
        ],
        out_specs=[
            pl.BlockSpec((pieces, 1, rows, 2 * HD), lambda g: (g % per_y, g // per_y, 0, 0)),
            pl.BlockSpec((1, rows, rows), lambda g: (g, 0, 0)),
        ],
        out_shape=[
            jax.ShapeDtypeStruct((z_size, y_size, rows, 2 * HD), F32),
            jax.ShapeDtypeStruct((groups, rows, rows), F32),
        ],
        scratch_shapes=[pltpu.VMEM((heads, rows), F32), pltpu.VMEM((heads, rows), F32)],
        compiler_params=pltpu.CompilerParams(vmem_limit_bytes=LIMIT),
        cost_estimate=pl.CostEstimate(
            flops=4 * heads * rows * HD, bytes_accessed=7 * 2**20, transcendentals=sources * heads * rows
        ),
        name="query_terms",
    )(stats, own, maxima, at, bt)


def image_kernel(core_ref, factor_ref, q_ref, do_ref, e_ref, es_ref, keep_k, keep_v, send_k, send_v):
    heads = q_ref.shape[1] // HD
    wide_rhs, narrow_rhs = [], []
    for h in range(heads):
        w = factor_ref[0, :, h : h + 1]
        wd = factor_ref[0, :, heads + h : heads + h + 1]
        q = head(q_ref, h).astype(F32)
        do = head(do_ref, h).astype(F32)
        wide_rhs.append(jnp.concatenate([(w * do).astype(BF16), (wd * q).astype(BF16)], axis=1))
        narrow_rhs.append((w * q).astype(BF16))
    both = jnp.dot(e_ref[...], jnp.concatenate(wide_rhs, axis=0), preferred_element_type=F32)
    rest = jnp.dot(es_ref[...], jnp.concatenate(narrow_rhs, axis=0), preferred_element_type=F32)
    grad_v = both[:, :HD]
    grad_k = (both[:, HD:] + rest) * SCALE
    even_core = core_ref[0] == 0
    pieces, size = keep_k.shape[0], keep_k.shape[1]
    for grad, keep_out, send_out in ((grad_k, keep_k, send_k), (grad_v, keep_v, send_v)):
        for piece in range(pieces):
            even = grad[2 * piece * size : (2 * piece + 1) * size]
            odd = grad[(2 * piece + 1) * size : (2 * piece + 2) * size]
            keep_out[piece] = jnp.where(even_core, even, odd)
            send_out[piece] = jnp.where(even_core, odd, even)


def image_part(core, factors, queries, grad_out, e, es, pieces):
    rows, width = queries.shape
    image_rows, wide = e.shape
    groups = factors.shape[0]
    per_group = width // groups
    size = image_rows // (2 * pieces)
    out = jax.ShapeDtypeStruct((pieces, size, groups * HD), F32)
    out_spec = pl.BlockSpec((pieces, size, HD), lambda g: (0, 0, g))
    return pl.pallas_call(
        image_kernel,
        grid=(groups,),
        in_specs=[
            pl.BlockSpec(memory_space=pltpu.SMEM),
            pl.BlockSpec((1, rows, rows), lambda g: (g, 0, 0)),
            pl.BlockSpec((rows, per_group), lambda g: (0, g)),
            pl.BlockSpec((rows, per_group), lambda g: (0, g)),
            pl.BlockSpec((image_rows, wide // groups), lambda g: (0, g)),
            pl.BlockSpec((image_rows, wide // groups), lambda g: (0, g)),
        ],
        out_specs=[out_spec] * 4,
        out_shape=[out] * 4,
        compiler_params=pltpu.CompilerParams(vmem_limit_bytes=LIMIT),
        cost_estimate=pl.CostEstimate(
            flops=6 * width * rows * image_rows, bytes_accessed=15 * 2**20, transcendentals=0
        ),
        name="image_terms",
    )(core, factors, queries, grad_out, e, es)


def on_device(queries, keys, values, grad_out, keep_blocks):
    image_size = lax.axis_size("image")
    text_size = lax.axis_size("text")
    y_size = 2
    z_size = image_size // y_size
    pieces = text_size // 2
    z_groups = [[y * z_size + z for z in range(z_size)] for y in range(y_size)]
    core_groups = [[2 * k + c for k in range(pieces)] for c in range(2)]
    image_index = lax.axis_index("image")
    core = lax.axis_index("text") % 2

    e, es, at, bt, own, maxima = local_part(keep_blocks, queries, grad_out, keys, values, image_size)
    stats = lax.all_to_all(own, "image", 0, 0, tiled=True)
    query_terms, factors = query_part(stats, own, maxima, at, bt, z_size, y_size)
    over_z = lax.psum_scatter(
        query_terms, "image", scatter_dimension=0, tiled=True, axis_index_groups=z_groups
    )[0]

    keep_k, keep_v, send_k, send_v = image_part(
        core.astype(jnp.int32).reshape(1), factors, queries, grad_out, e, es, pieces
    )
    swap_core = [(t, t ^ 1) for t in range(text_size)]
    image_terms = jnp.concatenate(
        [keep_k + lax.ppermute(send_k, "text", swap_core), keep_v + lax.ppermute(send_v, "text", swap_core)],
        axis=2,
    )
    arrived = lax.all_to_all(image_terms, "text", 0, 0, tiled=True, axis_index_groups=core_groups)
    image_sum = jnp.sum(arrived, axis=0)
    key_width = keys.shape[1]
    grad_keys = image_sum[:, :key_width].astype(BF16)
    grad_values = image_sum[:, key_width:].astype(BF16)

    mine = image_index // z_size
    own_y = lax.dynamic_index_in_dim(over_z, mine, 0, False)
    other_y = lax.dynamic_index_in_dim(over_z, 1 - mine, 0, False)
    swap_y = [(i, (i + z_size) % image_size) for i in range(image_size)]
    grad_queries = (own_y + lax.ppermute(other_y, "image", swap_y)).astype(BF16)
    return (grad_queries, grad_keys, grad_values)


def solution(mesh):
    return jax.shard_map(
        on_device,
        mesh=mesh,
        in_specs=(
            P("text", None),
            P("image", None),
            P("image", None),
            P("text", None),
            P("text", "image"),
        ),
        out_specs=(P("text", "image"), P(("image", "text"), None), P(("image", "text"), None)),
        check_vma=False,
    )
```

time: 358 us -> 108 us (0.30)
  waiting for transfers between devices: 132 us -> 27.1 us
  blocking collectives: 129 us -> 24.5 us
  Pallas kernels: 0 us -> 28.1 us
  matrix products: 27.1 us -> 0 us
  other arithmetic: 27.7 us -> 4.13 us
  local copies, waits for them, and re-layouts: 22.7 us -> 1.55 us
  starting transfers between devices: 0.3 us -> 7.68 us
    reduce_scatter x1, waiting for transfers between devices: 74.2 us -> 1.53 us  [on_device(): lax.psum_scatter(query_terms, 'image', scatter_dimension=0, tiled=True, a...]
    all_gather x2 -> x0, blocking collectives: 67.6 us -> none  [merged(): gathered = jax.tree.map(lambda a: lax.all_gather(a, axis), part)]
    psum x1 -> x0, blocking collectives: 61.9 us -> none  [on_device(): delta = lax.psum(jnp.concatenate(partial_delta, axis=0), 'image')]
    unnamed x5 -> x1, waiting for transfers between devices: 58.2 us -> 0.02 us
    pallas_call x0 -> x3, Pallas kernels: none -> 28.1 us  [the longest x1 14.9 us: local_part(): pl.pallas_call(local_kernel, grid=(groups,), in_specs=[pl.BlockSpec(memor...]
    dot_general x20 -> x0, matrix products: 27.1 us -> none  [the longest x4 8.54 us: value_products(): jnp.einsum('thd,kd->htk', grad_group, value_group, preferred_element_type...]
    all_to_all x0 -> x1, blocking collectives: none -> 24.5 us  [on_device(): stats = lax.all_to_all(own, 'image', 0, 0, tiled=True)]
    all_to_all x0 -> x1, waiting for transfers between devices: none -> 20.3 us  [on_device(): lax.all_to_all(image_terms, 'text', 0, 0, tiled=True, axis_index_groups=c...]
  transfers between devices with their start and end apart: 3 -> 5, of which waited for: 2 -> 4; matrix products, arithmetic and copies ran while one was open for 10% -> 3% of each run, Pallas kernels for 0% -> 8%
where the time goes in v1:
time: 108 us; the launch traced here: 107 us
  Pallas kernels  28.1 us (26%)
  waiting for transfers between devices  27.1 us (25%)
  blocking collectives  24.5 us (23%)
  between operations  14.1 us (13%)
  starting transfers between devices  7.68 us (7%)
  other arithmetic  4.13 us (4%)
  local copies, waits for them, and re-layouts  1.55 us (1%)
    all_to_all x1, blocking collectives, on_device(): stats = lax.all_to_all(own, 'image', 0, 0, tiled=True)  24.5 us
    all_to_all x1, waiting for transfers between devices, on_device(): lax.all_to_all(image_terms, 'text', 0, 0, tiled=True, axis_index_groups=c...  20.3 us
    pallas_call x1, Pallas kernels, local_part(): pl.pallas_call(local_kernel, grid=(groups,), in_specs=[pl.BlockSpec(memor...  14.9 us
    pallas_call x1, Pallas kernels, image_part(): pl.pallas_call(image_kernel, grid=(groups,), in_specs=[pl.BlockSpec(memor...  8.29 us
    all_to_all x1, starting transfers between devices, on_device(): lax.all_to_all(image_terms, 'text', 0, 0, tiled=True, axis_index_groups=c...  6.04 us
    pallas_call x1, Pallas kernels, query_part(): pl.pallas_call(query_kernel, grid=(groups,), in_specs=[pl.BlockSpec((sour...  4.87 us
    ppermute x1, waiting for transfers between devices, on_device(): grad_queries = (own_y + lax.ppermute(other_y, 'image', swap_y)).astype(BF16)  3.41 us
  transfers between devices with their start and end apart: 5, of which 4 were waited for; matrix products, arithmetic and copies ran while one was open for 3% of the time, Pallas kernels for 8%

profile of v1, /device:TPU:8, one launch (start us, length us, event | category | flops | bytes accessed | tf_op | source)
XLA Modules:
  0.0 107.2 jit_solution(1877324488215571688)
XLA Ops:
  7.2 0.0 reduce-scatter.2.cloned.1.call-start
  7.2 14.9 %local_products.1 = (bf16[640,4096]{1,0:T(8,128)(2,1)}, bf16[640,4096]{1,0:T(8,128)(2,1)}, f32[128,4096]{1,0:T(8,128)}, f32[128,4096]{1,0:T(8,128)}, f32[16,64,128]{2,1,0:T(8,128)}, /*index=5*/f32[32,128]{1,0:T(8,128)}) custom-call(s32[2,5]{1,0:T(2,128)} %keep_ref.1, bf16[128,4096]{1,0:T(8,128)(2,1)} %q_ref.3, bf16[128,4096]{1,0:T(8,128)(2,1)} %do_ref.3, ...), custom_call_target="tpu_custom_call" | custom-call | flops 2684354560 | bytes 18874368 | tf_op jit(solution)/shard_map/local_products/pallas_call | solution.py:119
  22.2 24.5 %all_to_all.10.all_ref = f32[16,64,128]{2,1,0:T(8,128)} all-to-all(f32[16,64,128]{2,1,0:T(8,128)} %get-tuple-element.15.own_ref), channel_id=1, replica_groups=mesh['text'=16,'image'=16] {'image'}, dimensions={0} | all-to-all | bytes 1048576 | tf_op jit(solution)/shard_map/all_to_all | solution.py:290
  46.7 4.9 %query_terms.1 = (f32[8,2,128,256]{3,2,1,0:T(8,128)}, f32[4,128,128]{2,1,0:T(8,128)}) custom-call(f32[16,64,128]{2,1,0:T(8,128)} %all_to_all.10.all_ref, f32[16,64,128]{2,1,0:T(8,128)} %get-tuple-element.15.own_ref, f32[32,128]{1,0:T(8,128)} %get-tuple-element.16.max_ref, f32[128,4096]{1,0:T(8,128)} %get-tuple-element.17.at_ref, ...), custom_call_target="tpu_custom_call" | custom-call | flops 2097152 | bytes 7340032 | tf_op jit(solution)/shard_map/query_terms/pallas_call | solution.py:198
  51.6 0.0 reduce-scatter.2.cloned.1.call-update
  51.6 8.3 %image_terms.1 = (f32[8,40,512]{2,1,0:T(8,128)}, f32[8,40,512]{2,1,0:T(8,128)}, f32[8,40,512]{2,1,0:T(8,128)}, f32[8,40,512]{2,1,0:T(8,128)}) custom-call(s32[1]{0:T(128)} %bitcast.2.core_ref, f32[4,128,128]{2,1,0:T(8,128)} %get-tuple-element.20.factor_ref, bf16[128,4096]{1,0:T(8,128)(2,1)} %q_ref.3, bf16[128,4096]{1,0:T(8,128)(2,1)} %do_ref.3, ...), custom_call_target="tpu_custom_call" | custom-call | flops 2013265920 | bytes 15728640 | tf_op jit(solution)/shard_map/image_terms/pallas_call | solution.py:257
  59.9 0.0 copy-start
  59.9 0.1 collective-permute-start.2
  60.0 0.5 collective-permute-start.1
  60.5 1.8 %collective-permute-done.2 = f32[8,40,512]{2,1,0:T(8,128)S(1)} collective-permute-done((f32[8,40,512]{2,1,0:T(8,128)}, f32[8,40,512]{2,1,0:T(8,128)S(1)}, u32[]{:S(2)}, u32[]{:S(2)}) %collective-permute-start.2) | collective-permute-done | bytes 655392 | tf_op jit(solution)/shard_map/ppermute | solution.py:301
  62.3 1.2 %add.29 = f32[8,40,512]{2,1,0:T(8,128)S(1)} add(f32[8,40,512]{2,1,0:T(8,128)} %get-tuple-element.25, f32[8,40,512]{2,1,0:T(8,128)S(1)} %collective-permute-done.2) | non-fusion elementwise | flops 163840 | bytes 1966080 | tf_op jit(solution)/shard_map/add | solution.py:301
  63.5 0.0 collective-permute-done.1
  63.5 0.0 copy-done
  63.5 0.1 add.28
  63.6 1.2 %pad_maximum_fusion = f32[8,40,1024]{2,1,0:T(8,128)} fusion(f32[8,40,512]{2,1,0:T(8,128)S(1)} %add.29, f32[8,40,512]{2,1,0:T(8,128)S(1)} %add.28), kind=kLoop, calls=%fused_computation | loop fusion | flops 327680 | bytes 2621440 | tf_op jit(solution)/shard_map/concatenate | solution.py:300
  64.8 6.0 %all-to-all-start.1 = ((f32[8,40,1024]{2,1,0:T(8,128)}), f32[8,40,1024]{2,1,0:T(8,128)S(1)}, u32[]{:S(2)}, u32[]{:S(2)}) async-start(f32[8,40,1024]{2,1,0:T(8,128)} %pad_maximum_fusion), calls=%async_computation.2 | async-start | bytes 2621440 | tf_op jit(solution)/shard_map/all_to_all | solution.py:304
  70.9 20.3 %all-to-all-done.1 = f32[8,40,1024]{2,1,0:T(8,128)S(1)} async-done(((f32[8,40,1024]{2,1,0:T(8,128)}), f32[8,40,1024]{2,1,0:T(8,128)S(1)}, u32[]{:S(2)}, u32[]{:S(2)}) %all-to-all-start.1) | async-done | bytes 1310752 | tf_op jit(solution)/shard_map/all_to_all | solution.py:304
  91.2 0.1 reduce_sum.9
  91.3 1.5 %reduce-scatter.2.cloned.1.call-done = f32[1,2,128,256]{3,2,1,0:T(8,128)} async-done(((f32[8,2,128,256]{3,2,1,0:T(8,128)}), f32[1,2,128,256]{3,2,1,0:T(8,128)}) %reduce-scatter.2.cloned.1.call-update) | async-done | bytes 262160 | tf_op jit(solution)/shard_map/reduce_scatter | solution.py:292
  92.8 0.9 dynamic-slice_bitcast_fusion
  93.7 1.0 collective-permute-start
  94.7 0.6 fusion.1
  95.4 3.4 %collective-permute-done = f32[128,256]{1,0:T(8,128)S(1)} collective-permute-done((f32[128,256]{1,0:T(8,128)S(1)}, f32[128,256]{1,0:T(8,128)S(1)}, u32[]{:S(2)}, u32[]{:S(2)}) %collective-permute-start) | collective-permute-done | bytes 131104 | tf_op jit(solution)/shard_map/ppermute | solution.py:314
  98.8 1.6 %fusion = bf16[128,256]{1,0:T(8,128)(2,1)} fusion(f32[128,256]{1,0:T(8,128)S(1)} %collective-permute-done, f32[1,2,128,256]{3,2,1,0:T(8,128)} %reduce-scatter.2.cloned.1.call-done, s32[]{:T(128)S(6)} %select_n.19), kind=kLoop, calls=%fused_computation.2 | loop fusion | flops 65536 | bytes 327684 | tf_op jit(solution)/shard_map/convert_element_type | solution.py:314
Async XLA Ops:
  7.2 85.6 %reduce-scatter.2.cloned.1.call-start = ((), (), s32[]{:S(2)}) async-start(), calls=%async_computation.3 | async-start | bytes 2359296 | tf_op jit(solution)/shard_map/reduce_scatter | solution.py:292
  59.9 3.6 %copy-start = (f32[8,40,512]{2,1,0:T(8,128)S(1)}, f32[8,40,512]{2,1,0:T(8,128)}, u32[]{:S(2)}) copy-start(f32[8,40,512]{2,1,0:T(8,128)} %get-tuple-element.23) | copy-start | bytes 1966084
  59.9 2.4 %collective-permute-start.2 = (f32[8,40,512]{2,1,0:T(8,128)}, f32[8,40,512]{2,1,0:T(8,128)S(1)}, u32[]{:S(2)}, u32[]{:S(2)}) collective-permute-start(f32[8,40,512]{2,1,0:T(8,128)} %get-tuple-element.26), channel_id=1, source_target_pairs={{0,16},{16,0},{32,48},{48,32},{64,80},{80,64},{96,112},{112,96},{1... | collective-permute-start | bytes 1966088 | tf_op jit(solution)/shard_map/ppermute | solution.py:301
  60.0 3.5 %collective-permute-start.1 = (f32[8,40,512]{2,1,0:T(8,128)}, f32[8,40,512]{2,1,0:T(8,128)S(1)}, u32[]{:S(2)}, u32[]{:S(2)}) collective-permute-start(f32[8,40,512]{2,1,0:T(8,128)} %get-tuple-element.24), channel_id=1, source_target_pairs={{0,16},{16,0},{32,48},{48,32},{64,80},{80,64},{96,112},{112,96},{1... | collective-permute-start | bytes 1966088 | tf_op jit(solution)/shard_map/ppermute | solution.py:301
  64.8 26.4 %all-to-all-start.1 = ((f32[8,40,1024]{2,1,0:T(8,128)}), f32[8,40,1024]{2,1,0:T(8,128)S(1)}, u32[]{:S(2)}, u32[]{:S(2)}) async-start(f32[8,40,1024]{2,1,0:T(8,128)} %pad_maximum_fusion), calls=%async_computation.2 | async-start | bytes 2621440 | tf_op jit(solution)/shard_map/all_to_all | solution.py:304
  93.7 5.1 %collective-permute-start = (f32[128,256]{1,0:T(8,128)S(1)}, f32[128,256]{1,0:T(8,128)S(1)}, u32[]{:S(2)}, u32[]{:S(2)}) collective-permute-start(f32[128,256]{1,0:T(8,128)S(1)} %dynamic-slice_bitcast_fusion), channel_id=1, source_target_pairs={{0,8},{1,9},{2,10},{3,11},{4,12},{5,13},{6,14},{7,15},{8,0},{9,1},... | collective-permute-start | bytes 393224 | tf_op jit(solution)/shard_map/ppermute | solution.py:314
Sparse Core Ops, SparseCore 0:
  51.7 41.0 reduce-scatter.1

commit v2 on v1

v2 whole, which is shorter than its diff:
```python
import jax
import jax.numpy as jnp
from jax import lax
from jax.experimental import pallas as pl
from jax.experimental.pallas import tpu as pltpu
from jax.sharding import PartitionSpec as P

HD = 128
TBLK = 64
FBLK = 128
SCALE = HD ** (-0.5)
MASKED = -1e30
NO_KEY = -1e29
LIMIT = 56 * 1024 * 1024

F32 = jnp.float32
BF16 = jnp.bfloat16
LAST = (((1,), (1,)), ((), ()))
FIRST = (((0,), (0,)), ((), ()))


def head(array, index):
    return array[:, index * HD : (index + 1) * HD]


def row_fold(block, combine):
    parts = [block[8 * i : 8 * i + 8] for i in range(block.shape[0] // 8)]
    while len(parts) > 1:
        parts = [combine(parts[i], parts[i + 1]) for i in range(0, len(parts) - 1, 2)] + (
            [parts[-1]] if len(parts) % 2 else []
        )
    return parts[0]


def local_kernel(keep_ref, q_ref, do_ref, k_ref, v_ref, e_ref, stat_ref, max_ref, s_scr, g_scr):
    group = pl.program_id(0)
    heads = q_ref.shape[1] // HD
    rows = q_ref.shape[0]
    blocks = k_ref.shape[0] // FBLK
    copies, stat_rows = stat_ref.shape[0], stat_ref.shape[1] // 2
    first_half = lax.broadcasted_iota(jnp.int32, (1, rows), 1) < TBLK
    bias = [
        jnp.where(
            first_half,
            jnp.where(keep_ref[0, b] > 0, 0.0, MASKED),
            jnp.where(keep_ref[1, b] > 0, 0.0, MASKED),
        ).astype(F32)
        for b in range(blocks)
    ]
    q_all = jnp.concatenate([head(q_ref, h) for h in range(heads)], axis=0)
    do_all = jnp.concatenate([head(do_ref, h) for h in range(heads)], axis=0)
    s_scr[...] = lax.dot_general(k_ref[...], q_all, LAST, preferred_element_type=F32)
    g_scr[...] = lax.dot_general(v_ref[...], do_all, LAST, preferred_element_type=F32)

    def block(h, b):
        return slice(b * FBLK, (b + 1) * FBLK), slice(h * rows, (h + 1) * rows)

    tops = []
    for h in range(heads):
        top = None
        for b in range(blocks):
            part = row_fold(s_scr[block(h, b)], jnp.maximum) + bias[b]
            top = part if top is None else jnp.maximum(top, part)
        tops.append(top)
    row_maxima = [jnp.maximum(jnp.max(top, axis=0, keepdims=True), NO_KEY) for top in tops]
    sums = []
    for h, row_max in enumerate(row_maxima):
        total = jnp.zeros((8, rows), F32)
        product = jnp.zeros((8, rows), F32)
        for b in range(blocks):
            weight = jnp.exp((s_scr[block(h, b)] + (bias[b] - row_max)) * SCALE)
            e_ref[block(h, b)] = weight.astype(BF16)
            total = total + row_fold(weight, jnp.add)
            product = product + row_fold(weight * g_scr[block(h, b)], jnp.add)
        sums.append((total, product))
    maxima, logs, deltas = [], [], []
    for (total, product), row_max in zip(sums, row_maxima):
        total = jnp.sum(total, axis=0, keepdims=True)
        product = jnp.sum(product, axis=0, keepdims=True)
        some = total > 0.0
        safe = jnp.where(some, total, 1.0)
        scaled_max = row_max * SCALE
        maxima.append(scaled_max)
        logs.append(jnp.where(some, scaled_max + jnp.log(safe), MASKED))
        deltas.append(product / safe)
    log_rows = jnp.concatenate(logs, axis=0)
    delta_rows = jnp.concatenate(deltas, axis=0)
    at = pl.multiple_of(group * heads, 8)
    for copy in range(copies):
        stat_ref[copy, pl.ds(at, heads), :] = log_rows
        stat_ref[copy, pl.ds(at + stat_rows, heads), :] = delta_rows
    max_ref[pl.ds(at, heads), :] = jnp.concatenate(maxima, axis=0)


def local_part(keep_blocks, queries, grad_out, keys, values, copies):
    rows, width = queries.shape
    image_rows, key_width = keys.shape
    groups = key_width // HD
    per_group = width // groups
    heads = width // HD
    wide_block = per_group // HD * rows
    return pl.pallas_call(
        local_kernel,
        grid=(groups,),
        in_specs=[
            pl.BlockSpec(memory_space=pltpu.SMEM),
            pl.BlockSpec((rows, per_group), lambda g: (0, g)),
            pl.BlockSpec((rows, per_group), lambda g: (0, g)),
            pl.BlockSpec((image_rows, HD), lambda g: (0, g)),
            pl.BlockSpec((image_rows, HD), lambda g: (0, g)),
        ],
        out_specs=[
            pl.BlockSpec((image_rows, wide_block), lambda g: (0, g)),
            pl.BlockSpec((copies, 2 * heads, rows), lambda g: (0, 0, 0)),
            pl.BlockSpec((heads, rows), lambda g: (0, 0)),
        ],
        out_shape=[
            jax.ShapeDtypeStruct((image_rows, groups * wide_block), BF16),
            jax.ShapeDtypeStruct((copies, 2 * heads, rows), F32),
            jax.ShapeDtypeStruct((heads, rows), F32),
        ],
        scratch_shapes=[
            pltpu.VMEM((image_rows, wide_block), F32),
            pltpu.VMEM((image_rows, wide_block), F32),
        ],
        compiler_params=pltpu.CompilerParams(vmem_limit_bytes=LIMIT),
        cost_estimate=pl.CostEstimate(
            flops=4 * width * rows * image_rows,
            bytes_accessed=9 * 2**20,
            transcendentals=heads * rows * image_rows,
        ),
        name="local_statistics",
    )(keep_blocks, queries, grad_out, keys, values)


def product_kernel(own_ref, do_ref, k_ref, v_ref, e_ref, es_ref, at_ref, bt_ref):
    heads = do_ref.shape[1] // HD
    rows = do_ref.shape[0]
    blocks = k_ref.shape[0] // FBLK
    do_all = jnp.concatenate([head(do_ref, h) for h in range(heads)], axis=0)
    grad_probs = lax.dot_general(v_ref[...], do_all, LAST, preferred_element_type=F32)
    for h in range(heads):
        lanes = slice(h * rows, (h + 1) * rows)
        delta = own_ref[0, h : h + 1, :]
        for b in range(blocks):
            block_rows = slice(b * FBLK, (b + 1) * FBLK)
            centred = (grad_probs[block_rows, lanes] - delta).astype(BF16)
            es_ref[block_rows, lanes] = e_ref[block_rows, lanes] * centred
    at_ref[...] = lax.dot_general(k_ref[...], es_ref[...], FIRST, preferred_element_type=F32)
    bt_ref[...] = lax.dot_general(k_ref[...], e_ref[...], FIRST, preferred_element_type=F32)


def product_part(own, grad_out, keys, values, e):
    rows, width = grad_out.shape
    image_rows, key_width = keys.shape
    groups = key_width // HD
    per_group = width // groups
    heads = per_group // HD
    wide_block = heads * rows
    wide = jax.ShapeDtypeStruct((HD, groups * wide_block), F32)
    return pl.pallas_call(
        product_kernel,
        grid=(groups,),
        in_specs=[
            pl.BlockSpec((1, heads, rows), lambda g: (0, groups + g, 0)),
            pl.BlockSpec((rows, per_group), lambda g: (0, g)),
            pl.BlockSpec((image_rows, HD), lambda g: (0, g)),
            pl.BlockSpec((image_rows, HD), lambda g: (0, g)),
            pl.BlockSpec((image_rows, wide_block), lambda g: (0, g)),
        ],
        out_specs=[
            pl.BlockSpec((image_rows, wide_block), lambda g: (0, g)),
            pl.BlockSpec((HD, wide_block), lambda g: (0, g)),
            pl.BlockSpec((HD, wide_block), lambda g: (0, g)),
        ],
        out_shape=[jax.ShapeDtypeStruct(e.shape, BF16), wide, wide],
        compiler_params=pltpu.CompilerParams(vmem_limit_bytes=LIMIT),
        cost_estimate=pl.CostEstimate(
            flops=6 * width * rows * image_rows, bytes_accessed=18 * 2**20, transcendentals=0
        ),
        name="local_products",
    )(own, grad_out, keys, values, e)


def piece_offsets(z_size):
    half = z_size // 2
    order = [half]
    for distance in range(half - 1, 0, -1):
        order += [-distance, distance]
    return order + [0]


def put_term(out_ref, y_slot, w_pair, d_pair, at_ref, bt_ref):
    rows = at_ref.shape[1] // 2
    for h in range(2):
        lanes = slice(h * rows, (h + 1) * rows)
        total = w_pair[h : h + 1] * at_ref[:, lanes] + d_pair[h : h + 1] * bt_ref[:, lanes]
        out_ref[y_slot, :, h * HD : (h + 1) * HD] = jnp.transpose(total * SCALE)


def merge_kernel(
    place_ref, all_ref, own_ref, max_ref, at0, at1, bt0, bt1,
    right_ref, left_ref, factor_ref, row_ref, row_scr,
):
    step = pl.program_id(0)
    sources, double, rows = all_ref.shape
    heads = double // 2
    pairs = heads // 2
    groups = factor_ref.shape[0]
    per_group = heads // groups

    @pl.when(step == 0)
    def _():
        logs = [all_ref[s, 0:heads, :] for s in range(sources)]
        top = logs[0]
        for log in logs[1:]:
            top = jnp.maximum(top, log)
        total = jnp.zeros((heads, rows), F32)
        product = jnp.zeros((heads, rows), F32)
        for s in range(sources):
            share = jnp.exp(logs[s] - top)
            total = total + share
            product = product + share * all_ref[s, heads:double, :]
        w = jnp.exp(max_ref[...] - (top + jnp.log(total)))
        d = w * (own_ref[0, heads:double, :] - product / total)
        for pair in range(pairs):
            both = jnp.concatenate([w[2 * pair : 2 * pair + 2], d[2 * pair : 2 * pair + 2]], axis=0)
            row_scr[pair, 0:4] = both
            row_ref[pair, 0:4] = both
        fill = jnp.zeros((rows - 2 * per_group, rows), F32)
        for g in range(groups):
            at = slice(g * per_group, (g + 1) * per_group)
            factor_ref[g] = jnp.transpose(jnp.concatenate([w[at], d[at], fill], axis=0))

    offset = jnp.where(step == 0, pairs // 4, pairs // 2 - pairs // 4 + 1)
    for slot, at_ref, bt_ref in ((0, at0, bt0), (1, at1, bt1)):
        pair_rows = row_scr[pair_at(place_ref, offset, slot, pairs)]

        @pl.when(step == 0)
        def _():
            put_term(right_ref, slot, pair_rows[0:2], pair_rows[2:4], at_ref, bt_ref)

        @pl.when(step == 1)
        def _():
            put_term(left_ref, slot, pair_rows[0:2], pair_rows[2:4], at_ref, bt_ref)


def pair_at(place_ref, offset, slot, pairs):
    z_size = pairs // 2
    y = lax.rem(place_ref[0] + slot, 2)
    return y * z_size + lax.rem(place_ref[1] + offset, z_size)


def merge_part(place, stats, own, maxima, at, bt, groups):
    sources, double, rows = stats.shape
    heads = double // 2
    pairs = heads // 2
    z_size = pairs // 2
    first, second = (o % z_size for o in piece_offsets(z_size)[:2])

    def spec(slot):
        def index(s, place):
            return 0, pair_at(place, jnp.where(s == 0, first, second), slot, pairs)

        return pl.BlockSpec((HD, 2 * rows), index)

    piece = jax.ShapeDtypeStruct((2, rows, 2 * HD), F32)
    piece_spec = pl.BlockSpec((2, rows, 2 * HD), lambda s, place: (0, 0, 0))
    grid_spec = pltpu.PrefetchScalarGridSpec(
        num_scalar_prefetch=1,
        grid=(2,),
        in_specs=[
            pl.BlockSpec((sources, double, rows), lambda s, place: (0, 0, 0)),
            pl.BlockSpec((1, double, rows), lambda s, place: (0, 0, 0)),
            pl.BlockSpec((heads, rows), lambda s, place: (0, 0)),
            spec(0), spec(1), spec(0), spec(1),
        ],
        out_specs=[
            piece_spec,
            piece_spec,
            pl.BlockSpec((groups, rows, rows), lambda s, place: (0, 0, 0)),
            pl.BlockSpec((pairs, 8, rows), lambda s, place: (0, 0, 0)),
        ],
        scratch_shapes=[pltpu.VMEM((pairs, 8, rows), F32)],
    )
    return pl.pallas_call(
        merge_kernel,
        grid_spec=grid_spec,
        out_shape=[
            piece,
            piece,
            jax.ShapeDtypeStruct((groups, rows, rows), F32),
            jax.ShapeDtypeStruct((pairs, 8, rows), F32),
        ],
        compiler_params=pltpu.CompilerParams(vmem_limit_bytes=LIMIT),
        cost_estimate=pl.CostEstimate(
            flops=heads * rows * HD, bytes_accessed=3 * 2**20, transcendentals=sources * heads * rows
        ),
        name="merged_statistics",
    )(place, stats, own, maxima, at, at, bt, bt)


def query_kernel(offset_ref, place_ref, row_ref, at0, at1, bt0, bt1, *out_refs):
    step = pl.program_id(0)
    pairs = row_ref.shape[0]
    for slot, at_ref, bt_ref in ((0, at0, bt0), (1, at1, bt1)):
        pair_rows = row_ref[pair_at(place_ref, offset_ref[step], slot, pairs)]
        for index, out_ref in enumerate(out_refs):

            @pl.when(step == index)
            def _(out_ref=out_ref):
                put_term(out_ref, slot, pair_rows[0:2], pair_rows[2:4], at_ref, bt_ref)


def query_part(offsets, place, pair_rows, at, bt):
    pairs, _, rows = pair_rows.shape
    count = offsets.shape[0]

    def spec(slot):
        def index(s, offset, place):
            return 0, pair_at(place, offset[s], slot, pairs)

        return pl.BlockSpec((HD, 2 * rows), index)

    piece_spec = pl.BlockSpec((2, rows, 2 * HD), lambda s, offset, place: (0, 0, 0))
    grid_spec = pltpu.PrefetchScalarGridSpec(
        num_scalar_prefetch=2,
        grid=(count,),
        in_specs=[
            pl.BlockSpec((pairs, 8, rows), lambda s, offset, place: (0, 0, 0)),
            spec(0), spec(1), spec(0), spec(1),
        ],
        out_specs=[piece_spec] * count,
    )
    return pl.pallas_call(
        query_kernel,
        grid_spec=grid_spec,
        out_shape=[jax.ShapeDtypeStruct((2, rows, 2 * HD), F32)] * count,
        compiler_params=pltpu.CompilerParams(vmem_limit_bytes=LIMIT),
        cost_estimate=pl.CostEstimate(
            flops=4 * count * 4 * rows * HD, bytes_accessed=5 * 2**20, transcendentals=0
        ),
        name="query_terms",
    )(offsets, place, pair_rows, at, at, bt, bt)


def image_kernel(core_ref, factor_ref, q_ref, do_ref, e_ref, es_ref, keep_ref, send_ref):
    heads = q_ref.shape[1] // HD
    wide_rhs, narrow_rhs = [], []
    for h in range(heads):
        w = factor_ref[0, :, h : h + 1]
        wd = factor_ref[0, :, heads + h : heads + h + 1]
        q = head(q_ref, h).astype(F32)
        do = head(do_ref, h).astype(F32)
        wide_rhs.append(jnp.concatenate([(w * do).astype(BF16), (wd * q).astype(BF16)], axis=1))
        narrow_rhs.append((w * q).astype(BF16))
    both = jnp.dot(e_ref[...], jnp.concatenate(wide_rhs, axis=0), preferred_element_type=F32)
    rest = jnp.dot(es_ref[...], jnp.concatenate(narrow_rhs, axis=0), preferred_element_type=F32)
    grad_v = both[:, :HD]
    grad_k = (both[:, HD:] + rest) * SCALE
    even_core = core_ref[0] == 0
    pieces, size = keep_ref.shape[0], keep_ref.shape[1]
    for at, grad in ((0, grad_k), (HD, grad_v)):
        for piece in range(pieces):
            even = grad[2 * piece * size : (2 * piece + 1) * size]
            odd = grad[(2 * piece + 1) * size : (2 * piece + 2) * size]
            keep_ref[piece, :, at : at + HD] = jnp.where(even_core, even, odd)
            send_ref[piece, :, at : at + HD] = jnp.where(even_core, odd, even)


def image_part(core, factors, queries, grad_out, e, es, pieces):
    rows, width = queries.shape
    image_rows, wide = e.shape
    groups = factors.shape[0]
    per_group = width // groups
    size = image_rows // (2 * pieces)
    out = jax.ShapeDtypeStruct((pieces, size, groups * 2 * HD), F32)
    out_spec = pl.BlockSpec((pieces, size, 2 * HD), lambda g: (0, 0, g))
    return pl.pallas_call(
        image_kernel,
        grid=(groups,),
        in_specs=[
            pl.BlockSpec(memory_space=pltpu.SMEM),
            pl.BlockSpec((1, rows, rows), lambda g: (g, 0, 0)),
            pl.BlockSpec((rows, per_group), lambda g: (0, g)),
            pl.BlockSpec((rows, per_group), lambda g: (0, g)),
            pl.BlockSpec((image_rows, wide // groups), lambda g: (0, g)),
            pl.BlockSpec((image_rows, wide // groups), lambda g: (0, g)),
        ],
        out_specs=[out_spec] * 2,
        out_shape=[out] * 2,
        compiler_params=pltpu.CompilerParams(vmem_limit_bytes=LIMIT),
        cost_estimate=pl.CostEstimate(
            flops=6 * width * rows * image_rows, bytes_accessed=15 * 2**20, transcendentals=0
        ),
        name="image_terms",
    )(core, factors, queries, grad_out, e, es)


def chain(first_right, first_left, later, axis, z_size, y_size):
    def turn(by):
        return [
            (y * z_size + z, y * z_size + (z + by) % z_size) for y in range(y_size) for z in range(z_size)
        ]

    order = piece_offsets(z_size)[2:]
    term = dict(zip(order, later))
    right = lax.ppermute(first_right, axis, turn(1))
    left = lax.ppermute(first_left, axis, turn(-1))
    for distance in range(z_size // 2 - 1, 0, -1):
        right = lax.ppermute(right + term[distance], axis, turn(1))
        if distance > 1:
            left = lax.ppermute(left + term[1 - distance], axis, turn(-1))
    return left, right, term[0]


def on_device(queries, keys, values, grad_out, keep_blocks):
    image_size = lax.axis_size("image")
    text_size = lax.axis_size("text")
    y_size = 2
    z_size = image_size // y_size
    pieces = text_size // 2
    groups = keys.shape[1] // HD
    core_groups = [[2 * k + c for k in range(pieces)] for c in range(2)]
    swap_y = [(i, (i + z_size) % image_size) for i in range(image_size)]
    swap_core = [(t, t ^ 1) for t in range(text_size)]
    image_index = lax.axis_index("image").astype(jnp.int32)
    place = jnp.stack([image_index // z_size, image_index % z_size])
    offsets = jnp.array([o % z_size for o in piece_offsets(z_size)[2:]], jnp.int32)
    core = (lax.axis_index("text") % 2).astype(jnp.int32).reshape(1)

    e, own, maxima = local_part(keep_blocks, queries, grad_out, keys, values, image_size)
    stats = lax.all_to_all(own, "image", 0, 0, tiled=True)
    es, at, bt = product_part(own, grad_out, keys, values, e)
    first_right, first_left, factors, pair_rows = merge_part(place, stats, own, maxima, at, bt, groups)
    later = query_part(offsets, place, pair_rows, at, bt)
    left, right, here = chain(first_right, first_left, later, "image", z_size, y_size)
    query_sum = left + right + here
    grad_queries = (query_sum[0] + lax.ppermute(query_sum[1], "image", swap_y)).astype(BF16)

    keep, send = image_part(core, factors, queries, grad_out, e, es, pieces)
    image_terms = keep + lax.ppermute(send, "text", swap_core)
    text_arrived = lax.all_to_all(image_terms, "text", 0, 0, tiled=True, axis_index_groups=core_groups)
    image_sum = jnp.sum(text_arrived, axis=0)
    both = image_sum.reshape(image_sum.shape[0], groups, 2, HD)
    grad_keys = both[:, :, 0].reshape(-1, groups * HD).astype(BF16)
    grad_values = both[:, :, 1].reshape(-1, groups * HD).astype(BF16)
    return (grad_queries, grad_keys, grad_values)


def solution(mesh):
    return jax.shard_map(
        on_device,
        mesh=mesh,
        in_specs=(
            P("text", None),
            P("image", None),
            P("image", None),
            P("text", None),
            P("text", "image"),
        ),
        out_specs=(P("text", "image"), P(("image", "text"), None), P(("image", "text"), None)),
        check_vma=False,
    )
```

time: 108 us -> 96.3 us (0.89)
  blocking collectives: 24.5 us -> 0 us
  starting transfers between devices: 7.68 us -> 28.3 us
  between operations: 14.1 us -> 0.77 us
  Pallas kernels: 28.1 us -> 34.9 us
  waiting for transfers between devices: 27.1 us -> 23.7 us
    all_to_all x1 -> x0, blocking collectives: 24.5 us -> none  [on_device(): stats = lax.all_to_all(own, 'image', 0, 0, tiled=True)]
    all_to_all x1, waiting for transfers between devices: 20.3 us -> 0.01 us  [on_device(): lax.all_to_all(image_terms, 'text', 0, 0, tiled=True, axis_index_groups=c...]
    pallas_call x1 -> x3, Pallas kernels: 4.87 us -> 18.9 us  [the longest x1 8.82 us: product_part(): pl.pallas_call(product_kernel, grid=(groups,), in_specs=[pl.BlockSpec((1,...]
    ppermute x3 -> x9, waiting for transfers between devices: 5.21 us -> 18.7 us  [the longest x3 8.55 us: chain(): right = lax.ppermute(right + term[distance], axis, turn(1))]
    ppermute x3 -> x9, starting transfers between devices: 1.6 us -> 12.2 us  [the longest x2 5.7 us: chain(): left = lax.ppermute(left + term[1 - distance], axis, turn(-1))]
    all_to_all x0 -> x1, starting transfers between devices: none -> 9.95 us  [on_device(): stats = lax.all_to_all(own, 'image', 0, 0, tiled=True)]
    pallas_call x1, Pallas kernels: 14.9 us -> 7.56 us  [local_part(): pl.pallas_call(local_kernel, grid=(groups,), in_specs=[pl.BlockSpec(memor...]
    all_to_all x0 -> x1, waiting for transfers between devices: none -> 4.98 us  [on_device(): stats = lax.all_to_all(own, 'image', 0, 0, tiled=True)]
  transfers between devices with their start and end apart: 5 -> 11, of which waited for: 4 -> 6; matrix products, arithmetic and copies ran while one was open for 3% -> 5% of each run, Pallas kernels for 8% -> 16%
where the time goes in v2:
time: 96.3 us; the launch traced here: 94.6 us
  Pallas kernels  34.9 us (36%)
  starting transfers between devices  28.3 us (29%)
  waiting for transfers between devices  23.7 us (25%)
  other arithmetic  4.98 us (5%)
  local copies, waits for them, and re-layouts  1.98 us (2%)
    all_to_all x1, starting transfers between devices, on_device(): stats = lax.all_to_all(own, 'image', 0, 0, tiled=True)  9.95 us
    pallas_call x1, Pallas kernels, product_part(): pl.pallas_call(product_kernel, grid=(groups,), in_specs=[pl.BlockSpec((1,...  8.82 us
    ppermute x3, waiting for transfers between devices, chain(): right = lax.ppermute(right + term[distance], axis, turn(1))  8.55 us
    pallas_call x1, Pallas kernels, image_part(): pl.pallas_call(image_kernel, grid=(groups,), in_specs=[pl.BlockSpec(memor...  8.4 us
    pallas_call x1, Pallas kernels, local_part(): pl.pallas_call(local_kernel, grid=(groups,), in_specs=[pl.BlockSpec(memor...  7.56 us
    pallas_call x1, Pallas kernels, query_part(): pl.pallas_call(query_kernel, grid_spec=grid_spec, out_shape=[jax.ShapeDty...  6.38 us
    all_to_all x1, starting transfers between devices, on_device(): lax.all_to_all(image_terms, 'text', 0, 0, tiled=True, axis_index_groups=c...  6.16 us
    ppermute x1, waiting for transfers between devices, on_device(): lax.ppermute(query_sum[1], 'image', swap_y)  6.14 us
  transfers between devices with their start and end apart: 11, of which 6 were waited for; matrix products, arithmetic and copies ran while one was open for 5% of the time, Pallas kernels for 16%

profile of v2, /device:TPU:8, one launch (start us, length us, event | category | flops | bytes accessed | tf_op | source)
XLA Modules:
  0.0 94.6 jit_solution(18033927324283996297)
XLA Ops:
  0.6 7.6 %local_statistics.1 = (bf16[640,4096]{1,0:T(8,128)(2,1)}, f32[16,64,128]{2,1,0:T(8,128)}, f32[32,128]{1,0:T(8,128)}) custom-call(s32[2,5]{1,0:T(2,128)} %keep_ref.1, bf16[128,4096]{1,0:T(8,128)(2,1)} %q_ref.3, bf16[128,4096]{1,0:T(8,128)(2,1)} %do_ref.5, bf16[640,512]{1,0:T(8,128)(2,1)} %k_ref.3, bf16[640,512]{1,0:T(8,128)(2,1)} %v_ref.3), custom_call_target="tpu_custom_call" | custom-call | flops 1342177280 | bytes 9437184 | tf_op jit(solution)/shard_map/local_statistics/pallas_call | solution.py:102
  8.2 10.0 %all-to-all-start = ((f32[16,64,128]{2,1,0:T(8,128)}), f32[16,64,128]{2,1,0:T(8,128)S(1)}, u32[]{:S(2)}, u32[]{:S(2)}) async-start(f32[16,64,128]{2,1,0:T(8,128)} %get-tuple-element.21.own_ref), calls=%async_computation | async-start | bytes 1048576 | tf_op jit(solution)/shard_map/all_to_all | solution.py:433
  18.1 0.7 pad_add_fusion.place_ref
  18.8 8.8 %local_products.1 = (bf16[640,4096]{1,0:T(8,128)(2,1)}, f32[128,4096]{1,0:T(8,128)}, f32[128,4096]{1,0:T(8,128)}) custom-call(f32[16,64,128]{2,1,0:T(8,128)} %get-tuple-element.21.own_ref, bf16[128,4096]{1,0:T(8,128)(2,1)} %do_ref.5, bf16[640,512]{1,0:T(8,128)(2,1)} %k_ref.3, bf16[640,512]{1,0:T(8,128)(2,1)} %v_ref.3, bf16[640,4096]{1,0:T(8,128)(2,1)} %get-tuple-element.23.e_ref), custom_call_target="tpu_custom_call" | custom-call | flops 2013265920 | bytes 18874368 | tf_op jit(solution)/shard_map/local_products/pallas_call | solution.py:161
  27.6 5.0 %all-to-all-done.all_ref = f32[16,64,128]{2,1,0:T(8,128)S(1)} async-done(((f32[16,64,128]{2,1,0:T(8,128)}), f32[16,64,128]{2,1,0:T(8,128)S(1)}, u32[]{:S(2)}, u32[]{:S(2)}) %all-to-all-start) | async-done | bytes 524320 | tf_op jit(solution)/shard_map/all_to_all | solution.py:433
  32.6 0.8 copy-done
  33.4 3.7 %merged_statistics.1 = (f32[2,128,256]{2,1,0:T(8,128)}, f32[2,128,256]{2,1,0:T(8,128)}, f32[4,128,128]{2,1,0:T(8,128)}, f32[16,8,128]{2,1,0:T(8,128)}) custom-call(s32[2]{0:T(128)} %pad_add_fusion.place_ref, f32[16,64,128]{2,1,0:T(8,128)} %copy-done, f32[16,64,128]{2,1,0:T(8,128)} %get-tuple-element.21.own_ref, f32[32,128]{1,0:T(8,128)} %get-tuple-element.22.max_ref, ...), custom_call_target="tpu_custom_call" | custom-call | flops 524288 | bytes 3145728 | tf_op jit(solution)/shard_map/merged_statistics/pallas_call | solution.py:286
  37.2 8.4 %image_terms.1 = (f32[8,40,1024]{2,1,0:T(8,128)}, f32[8,40,1024]{2,1,0:T(8,128)}) custom-call(s32[1]{0:T(128)} %bitcast.4.core_ref, f32[4,128,128]{2,1,0:T(8,128)} %get-tuple-element.35.factor_ref, bf16[128,4096]{1,0:T(8,128)(2,1)} %q_ref.3, bf16[128,4096]{1,0:T(8,128)(2,1)} %do_ref.5, bf16[640,4096]{1,0:T(8,128)(2,1)} %get-tuple-element.23.e_ref, ...), custom_call_target="tpu_custom_call" | custom-call | flops 2013265920 | bytes 15728640 | tf_op jit(solution)/shard_map/image_terms/pallas_call | solution.py:379
  45.6 2.2 %collective-permute-start.3 = (f32[2,128,256]{2,1,0:T(8,128)S(1)}, f32[2,128,256]{2,1,0:T(8,128)S(1)}, u32[]{:S(2)}, u32[]{:S(2)}) collective-permute-start(f32[2,128,256]{2,1,0:T(8,128)S(1)} %copy-done.7), channel_id=1, source_target_pairs={{0,1},{1,2},{2,3},{3,4},{4,5},{5,6},{6,7},{7,0},{8,9},{9,10},{10,1... | collective-permute-start | bytes 786440 | tf_op jit(solution)/shard_map/ppermute | solution.py:408
  47.8 1.1 %collective-permute-start = (f32[2,128,256]{2,1,0:T(8,128)S(1)}, f32[2,128,256]{2,1,0:T(8,128)S(1)}, u32[]{:S(2)}, u32[]{:S(2)}) collective-permute-start(f32[2,128,256]{2,1,0:T(8,128)S(1)} %copy-done.6), channel_id=1, source_target_pairs={{0,7},{1,0},{2,1},{3,2},{4,3},{5,4},{6,5},{7,6},{8,15},{9,8},{10,9... | collective-permute-start | bytes 786440 | tf_op jit(solution)/shard_map/ppermute | solution.py:409
  48.9 6.4 %query_terms.1 = (f32[2,128,256]{2,1,0:T(8,128)}, f32[2,128,256]{2,1,0:T(8,128)}, f32[2,128,256]{2,1,0:T(8,128)}, f32[2,128,256]{2,1,0:T(8,128)}, f32[2,128,256]{2,1,0:T(8,128)}, /*index=5*/f32[2,128,256]{2,1,0:T(8,128)}) custom-call(s32[6]{0:T(128)} %constant.46.clone.offset_ref, s32[2]{0:T(128)} %pad_add_fusion.place_ref, ...), custom_call_target="tpu_custom_call" | custom-call | flops 1572864 | bytes 5242880 | tf_op jit(solution)/shard_map/query_terms/pallas_call | solution.py:335
  55.5 1.1 %add.38 = f32[2,128,256]{2,1,0:T(8,128)S(1)} add(f32[2,128,256]{2,1,0:T(8,128)S(1)} %collective-permute-done.3, f32[2,128,256]{2,1,0:T(8,128)} %get-tuple-element.31) | non-fusion elementwise | flops 65536 | bytes 786432 | tf_op jit(solution)/shard_map/add | solution.py:411
  56.6 1.0 %collective-permute-start.4 = (f32[2,128,256]{2,1,0:T(8,128)S(1)}, f32[2,128,256]{2,1,0:T(8,128)S(1)}, u32[]{:S(2)}, u32[]{:S(2)}) collective-permute-start(f32[2,128,256]{2,1,0:T(8,128)S(1)} %add.38), channel_id=1, source_target_pairs={{0,1},{1,2},{2,3},{3,4},{4,5},{5,6},{6,7},{7,0},{8,9},{9,10},{10,1... | collective-permute-start | bytes 786440 | tf_op jit(solution)/shard_map/ppermute | solution.py:411
  57.6 1.0 %add.36 = f32[2,128,256]{2,1,0:T(8,128)S(1)} add(f32[2,128,256]{2,1,0:T(8,128)S(1)} %collective-permute-done, f32[2,128,256]{2,1,0:T(8,128)} %get-tuple-element.28) | non-fusion elementwise | flops 65536 | bytes 786432 | tf_op jit(solution)/shard_map/add | solution.py:413
  58.6 2.4 %collective-permute-start.1 = (f32[2,128,256]{2,1,0:T(8,128)S(1)}, f32[2,128,256]{2,1,0:T(8,128)S(1)}, u32[]{:S(2)}, u32[]{:S(2)}) collective-permute-start(f32[2,128,256]{2,1,0:T(8,128)S(1)} %add.36), channel_id=1, source_target_pairs={{0,7},{1,0},{2,1},{3,2},{4,3},{5,4},{6,5},{7,6},{8,15},{9,8},{10,9... | collective-permute-start | bytes 786440 | tf_op jit(solution)/shard_map/ppermute | solution.py:413
  61.0 4.8 %collective-permute-done.4 = f32[2,128,256]{2,1,0:T(8,128)S(1)} collective-permute-done((f32[2,128,256]{2,1,0:T(8,128)S(1)}, f32[2,128,256]{2,1,0:T(8,128)S(1)}, u32[]{:S(2)}, u32[]{:S(2)}) %collective-permute-start.4) | collective-permute-done | bytes 262176 | tf_op jit(solution)/shard_map/ppermute | solution.py:411
  65.9 1.3 %add.45 = f32[8,40,1024]{2,1,0:T(8,128)} add(f32[8,40,1024]{2,1,0:T(8,128)S(1)} %copy-done.1, f32[8,40,1024]{2,1,0:T(8,128)S(1)} %collective-permute-done.8) | non-fusion elementwise | flops 327680 | bytes 3932160 | tf_op jit(solution)/shard_map/add | solution.py:442
  67.3 6.2 %all-to-all-start.1 = ((f32[8,40,1024]{2,1,0:T(8,128)}), f32[8,40,1024]{2,1,0:T(8,128)S(1)}, u32[]{:S(2)}, u32[]{:S(2)}) async-start(f32[8,40,1024]{2,1,0:T(8,128)} %add.45), calls=%async_computation.1 | async-start | bytes 2621440 | tf_op jit(solution)/shard_map/all_to_all | solution.py:443
  73.5 3.3 %collective-permute-start.2 = (f32[2,128,256]{2,1,0:T(8,128)S(1)}, f32[2,128,256]{2,1,0:T(8,128)S(1)}, u32[]{:S(2)}, u32[]{:S(2)}) collective-permute-start(f32[2,128,256]{2,1,0:T(8,128)S(1)} %add.37), channel_id=1, source_target_pairs={{0,7},{1,0},{2,1},{3,2},{4,3},{5,4},{6,5},{7,6},{8,15},{9,8},{10,9... | collective-permute-start | bytes 786440 | tf_op jit(solution)/shard_map/ppermute | solution.py:413
  76.9 3.8 %collective-permute-done.2 = f32[2,128,256]{2,1,0:T(8,128)S(1)} collective-permute-done((f32[2,128,256]{2,1,0:T(8,128)S(1)}, f32[2,128,256]{2,1,0:T(8,128)S(1)}, u32[]{:S(2)}, u32[]{:S(2)}) %collective-permute-start.2) | collective-permute-done | bytes 262176 | tf_op jit(solution)/shard_map/ppermute | solution.py:413
  80.7 3.8 %collective-permute-done.6 = f32[2,128,256]{2,1,0:T(8,128)S(1)} collective-permute-done((f32[2,128,256]{2,1,0:T(8,128)S(1)}, f32[2,128,256]{2,1,0:T(8,128)S(1)}, u32[]{:S(2)}, u32[]{:S(2)}) %collective-permute-start.6) | collective-permute-done | bytes 262176 | tf_op jit(solution)/shard_map/ppermute | solution.py:411
  84.6 2.0 %collective-permute-start.7 = (f32[128,256]{1,0:T(8,128)S(1)}, f32[128,256]{1,0:T(8,128)S(1)}, u32[]{:S(2)}, u32[]{:S(2)}) collective-permute-start(f32[128,256]{1,0:T(8,128)S(1)} %slice_bitcast_fusion), channel_id=1, source_target_pairs={{0,8},{1,9},{2,10},{3,11},{4,12},{5,13},{6,14},{7,15},{8,0},{9,1},... | collective-permute-start | bytes 393224 | tf_op jit(solution)/shard_map/ppermute | solution.py:439
  86.6 6.1 %collective-permute-done.7 = f32[128,256]{1,0:T(8,128)S(1)} collective-permute-done((f32[128,256]{1,0:T(8,128)S(1)}, f32[128,256]{1,0:T(8,128)S(1)}, u32[]{:S(2)}, u32[]{:S(2)}) %collective-permute-start.7) | collective-permute-done | bytes 131104 | tf_op jit(solution)/shard_map/ppermute | solution.py:439
  92.7 0.6 fusion.1
  (33 shorter events, 1.8 us)
Async XLA Ops:
  8.2 24.4 %all-to-all-start = ((f32[16,64,128]{2,1,0:T(8,128)}), f32[16,64,128]{2,1,0:T(8,128)S(1)}, u32[]{:S(2)}, u32[]{:S(2)}) async-start(f32[16,64,128]{2,1,0:T(8,128)} %get-tuple-element.21.own_ref), calls=%async_computation | async-start | bytes 1048576 | tf_op jit(solution)/shard_map/all_to_all | solution.py:433
  32.6 0.8 copy-start
  37.2 8.4 %copy-start.7 = (f32[2,128,256]{2,1,0:T(8,128)S(1)}, f32[2,128,256]{2,1,0:T(8,128)}, u32[]{:S(2)}) copy-start(f32[2,128,256]{2,1,0:T(8,128)} %get-tuple-element.30) | copy-start | bytes 786436
  37.2 10.6 %copy-start.6 = (f32[2,128,256]{2,1,0:T(8,128)S(1)}, f32[2,128,256]{2,1,0:T(8,128)}, u32[]{:S(2)}) copy-start(f32[2,128,256]{2,1,0:T(8,128)} %get-tuple-element.26) | copy-start | bytes 786436
  45.6 20.3 %collective-permute-start.8 = (f32[8,40,1024]{2,1,0:T(8,128)}, f32[8,40,1024]{2,1,0:T(8,128)S(1)}, u32[]{:S(2)}, u32[]{:S(2)}) collective-permute-start(f32[8,40,1024]{2,1,0:T(8,128)} %get-tuple-element.38), channel_id=1, source_target_pairs={{0,16},{16,0},{32,48},{48,32},{64,80},{80,64},{96,112},{112,96},{1... | collective-permute-start | bytes 3932168 | tf_op jit(solution)/shard_map/ppermute | solution.py:442
  45.6 9.9 %collective-permute-start.3 = (f32[2,128,256]{2,1,0:T(8,128)S(1)}, f32[2,128,256]{2,1,0:T(8,128)S(1)}, u32[]{:S(2)}, u32[]{:S(2)}) collective-permute-start(f32[2,128,256]{2,1,0:T(8,128)S(1)} %copy-done.7), channel_id=1, source_target_pairs={{0,1},{1,2},{2,3},{3,4},{4,5},{5,6},{6,7},{7,0},{8,9},{9,10},{10,1... | collective-permute-start | bytes 786440 | tf_op jit(solution)/shard_map/ppermute | solution.py:408
  47.8 9.8 %collective-permute-start = (f32[2,128,256]{2,1,0:T(8,128)S(1)}, f32[2,128,256]{2,1,0:T(8,128)S(1)}, u32[]{:S(2)}, u32[]{:S(2)}) collective-permute-start(f32[2,128,256]{2,1,0:T(8,128)S(1)} %copy-done.6), channel_id=1, source_target_pairs={{0,7},{1,0},{2,1},{3,2},{4,3},{5,4},{6,5},{7,6},{8,15},{9,8},{10,9... | collective-permute-start | bytes 786440 | tf_op jit(solution)/shard_map/ppermute | solution.py:409
  55.3 10.5 %copy-start.4 = (f32[2,128,256]{2,1,0:T(8,128)S(1)}, f32[2,128,256]{2,1,0:T(8,128)}, u32[]{:S(2)}) copy-start(f32[2,128,256]{2,1,0:T(8,128)} %get-tuple-element.32) | copy-start | bytes 786436
  55.3 10.6 %copy-start.1 = (f32[8,40,1024]{2,1,0:T(8,128)S(1)}, f32[8,40,1024]{2,1,0:T(8,128)}, u32[]{:S(2)}) copy-start(f32[8,40,1024]{2,1,0:T(8,128)} %get-tuple-element.37) | copy-start | bytes 3932164
  56.6 9.1 %collective-permute-start.4 = (f32[2,128,256]{2,1,0:T(8,128)S(1)}, f32[2,128,256]{2,1,0:T(8,128)S(1)}, u32[]{:S(2)}, u32[]{:S(2)}) collective-permute-start(f32[2,128,256]{2,1,0:T(8,128)S(1)} %add.38), channel_id=1, source_target_pairs={{0,1},{1,2},{2,3},{3,4},{4,5},{5,6},{6,7},{7,0},{8,9},{9,10},{10,1... | collective-permute-start | bytes 786440 | tf_op jit(solution)/shard_map/ppermute | solution.py:411
  58.6 14.9 %collective-permute-start.1 = (f32[2,128,256]{2,1,0:T(8,128)S(1)}, f32[2,128,256]{2,1,0:T(8,128)S(1)}, u32[]{:S(2)}, u32[]{:S(2)}) collective-permute-start(f32[2,128,256]{2,1,0:T(8,128)S(1)} %add.36), channel_id=1, source_target_pairs={{0,7},{1,0},{2,1},{3,2},{4,3},{5,4},{6,5},{7,6},{8,15},{9,8},{10,9... | collective-permute-start | bytes 786440 | tf_op jit(solution)/shard_map/ppermute | solution.py:413
  65.8 11.0 %collective-permute-start.5 = (f32[2,128,256]{2,1,0:T(8,128)S(1)}, f32[2,128,256]{2,1,0:T(8,128)S(1)}, u32[]{:S(2)}, u32[]{:S(2)}) collective-permute-start(f32[2,128,256]{2,1,0:T(8,128)S(1)} %add.39), channel_id=1, source_target_pairs={{0,1},{1,2},{2,3},{3,4},{4,5},{5,6},{6,7},{7,0},{8,9},{9,10},{10,1... | collective-permute-start | bytes 786440 | tf_op jit(solution)/shard_map/ppermute | solution.py:411
  67.3 6.2 %copy-start.3 = (f32[2,128,256]{2,1,0:T(8,128)S(1)}, f32[2,128,256]{2,1,0:T(8,128)}, u32[]{:S(2)}) copy-start(f32[2,128,256]{2,1,0:T(8,128)} %get-tuple-element.29) | copy-start | bytes 786436
  67.3 9.5 %copy-start.2 = (f32[2,128,256]{2,1,0:T(8,128)S(1)}, f32[2,128,256]{2,1,0:T(8,128)}, u32[]{:S(2)}) copy-start(f32[2,128,256]{2,1,0:T(8,128)} %get-tuple-element.33) | copy-start | bytes 786436
  67.3 26.1 %all-to-all-start.1 = ((f32[8,40,1024]{2,1,0:T(8,128)}), f32[8,40,1024]{2,1,0:T(8,128)S(1)}, u32[]{:S(2)}, u32[]{:S(2)}) async-start(f32[8,40,1024]{2,1,0:T(8,128)} %add.45), calls=%async_computation.1 | async-start | bytes 2621440 | tf_op jit(solution)/shard_map/all_to_all | solution.py:443
  73.4 11.1 %copy-start.5 = (f32[2,128,256]{2,1,0:T(8,128)S(1)}, f32[2,128,256]{2,1,0:T(8,128)}, u32[]{:S(2)}) copy-start(f32[2,128,256]{2,1,0:T(8,128)} %get-tuple-element.34) | copy-start | bytes 786436
  73.5 7.2 %collective-permute-start.2 = (f32[2,128,256]{2,1,0:T(8,128)S(1)}, f32[2,128,256]{2,1,0:T(8,128)S(1)}, u32[]{:S(2)}, u32[]{:S(2)}) collective-permute-start(f32[2,128,256]{2,1,0:T(8,128)S(1)} %add.37), channel_id=1, source_target_pairs={{0,7},{1,0},{2,1},{3,2},{4,3},{5,4},{6,5},{7,6},{8,15},{9,8},{10,9... | collective-permute-start | bytes 786440 | tf_op jit(solution)/shard_map/ppermute | solution.py:413
  76.8 7.7 %collective-permute-start.6 = (f32[2,128,256]{2,1,0:T(8,128)S(1)}, f32[2,128,256]{2,1,0:T(8,128)S(1)}, u32[]{:S(2)}, u32[]{:S(2)}) collective-permute-start(f32[2,128,256]{2,1,0:T(8,128)S(1)} %add.40), channel_id=1, source_target_pairs={{0,1},{1,2},{2,3},{3,4},{4,5},{5,6},{6,7},{7,0},{8,9},{9,10},{10,1... | collective-permute-start | bytes 786440 | tf_op jit(solution)/shard_map/ppermute | solution.py:411
  84.6 8.1 %collective-permute-start.7 = (f32[128,256]{1,0:T(8,128)S(1)}, f32[128,256]{1,0:T(8,128)S(1)}, u32[]{:S(2)}, u32[]{:S(2)}) collective-permute-start(f32[128,256]{1,0:T(8,128)S(1)} %slice_bitcast_fusion), channel_id=1, source_target_pairs={{0,8},{1,9},{2,10},{3,11},{4,12},{5,13},{6,14},{7,15},{8,0},{9,1},... | collective-permute-start | bytes 393224 | tf_op jit(solution)/shard_map/ppermute | solution.py:439

commit v3 on v2

--- a/solution.py
+++ b/solution.py
@@ -12,6 +12,9 @@
 MASKED = -1e30
 NO_KEY = -1e29
 LIMIT = 56 * 1024 * 1024
+PRODUCT_LIMIT = 56 * 1024 * 1024
+MERGE_LIMIT = 56 * 1024 * 1024
+TERM_LIMIT = 56 * 1024 * 1024
 
 F32 = jnp.float32
 BF16 = jnp.bfloat16
@@ -144,8 +147,8 @@
         delta = own_ref[0, h : h + 1, :]
         for b in range(blocks):
             block_rows = slice(b * FBLK, (b + 1) * FBLK)
-            centred = (grad_probs[block_rows, lanes] - delta).astype(BF16)
-            es_ref[block_rows, lanes] = e_ref[block_rows, lanes] * centred
+            centred = grad_probs[block_rows, lanes] - delta
+            es_ref[block_rows, lanes] = (e_ref[block_rows, lanes].astype(F32) * centred).astype(BF16)
     at_ref[...] = lax.dot_general(k_ref[...], es_ref[...], FIRST, preferred_element_type=F32)
     bt_ref[...] = lax.dot_general(k_ref[...], e_ref[...], FIRST, preferred_element_type=F32)
 
@@ -174,7 +177,7 @@
             pl.BlockSpec((HD, wide_block), lambda g: (0, g)),
         ],
         out_shape=[jax.ShapeDtypeStruct(e.shape, BF16), wide, wide],
-        compiler_params=pltpu.CompilerParams(vmem_limit_bytes=LIMIT),
+        compiler_params=pltpu.CompilerParams(vmem_limit_bytes=PRODUCT_LIMIT),
         cost_estimate=pl.CostEstimate(
             flops=6 * width * rows * image_rows, bytes_accessed=18 * 2**20, transcendentals=0
         ),
@@ -190,24 +193,24 @@
     return order + [0]
 
 
-def put_term(out_ref, y_slot, w_pair, d_pair, at_ref, bt_ref):
+def put_term(out_ref, y_slot, factor_ref, pair, at_ref, bt_ref):
     rows = at_ref.shape[1] // 2
     for h in range(2):
         lanes = slice(h * rows, (h + 1) * rows)
-        total = w_pair[h : h + 1] * at_ref[:, lanes] + d_pair[h : h + 1] * bt_ref[:, lanes]
-        out_ref[y_slot, :, h * HD : (h + 1) * HD] = jnp.transpose(total * SCALE)
+        w_row = factor_ref[0, pl.ds(2 * pair + h, 1), :]
+        d_row = factor_ref[1, pl.ds(2 * pair + h, 1), :]
+        out_ref[y_slot, :, h * HD : (h + 1) * HD] = jnp.transpose(
+            w_row * at_ref[:, lanes] + d_row * bt_ref[:, lanes]
+        )
 
 
 def merge_kernel(
-    place_ref, all_ref, own_ref, max_ref, at0, at1, bt0, bt1,
-    right_ref, left_ref, factor_ref, row_ref, row_scr,
+    place_ref, all_ref, own_ref, max_ref, at0, at1, bt0, bt1, right_ref, left_ref, factor_ref, row_scr
 ):
     step = pl.program_id(0)
     sources, double, rows = all_ref.shape
     heads = double // 2
     pairs = heads // 2
-    groups = factor_ref.shape[0]
-    per_group = heads // groups
 
     @pl.when(step == 0)
     def _():
@@ -223,26 +226,22 @@
             product = product + share * all_ref[s, heads:double, :]
         w = jnp.exp(max_ref[...] - (top + jnp.log(total)))
         d = w * (own_ref[0, heads:double, :] - product / total)
-        for pair in range(pairs):
-            both = jnp.concatenate([w[2 * pair : 2 * pair + 2], d[2 * pair : 2 * pair + 2]], axis=0)
-            row_scr[pair, 0:4] = both
-            row_ref[pair, 0:4] = both
-        fill = jnp.zeros((rows - 2 * per_group, rows), F32)
-        for g in range(groups):
-            at = slice(g * per_group, (g + 1) * per_group)
-            factor_ref[g] = jnp.transpose(jnp.concatenate([w[at], d[at], fill], axis=0))
+        factor_ref[0] = w
+        factor_ref[1] = d
+        row_scr[0] = w * SCALE
+        row_scr[1] = d * SCALE
 
     offset = jnp.where(step == 0, pairs // 4, pairs // 2 - pairs // 4 + 1)
     for slot, at_ref, bt_ref in ((0, at0, bt0), (1, at1, bt1)):
-        pair_rows = row_scr[pair_at(place_ref, offset, slot, pairs)]
+        pair = pair_at(place_ref, offset, slot, pairs)
 
         @pl.when(step == 0)
         def _():
-            put_term(right_ref, slot, pair_rows[0:2], pair_rows[2:4], at_ref, bt_ref)
+            put_term(right_ref, slot, row_scr, pair, at_ref, bt_ref)
 
         @pl.when(step == 1)
         def _():
-            put_term(left_ref, slot, pair_rows[0:2], pair_rows[2:4], at_ref, bt_ref)
+            put_term(left_ref, slot, row_scr, pair, at_ref, bt_ref)
 
 
 def pair_at(place_ref, offset, slot, pairs):
@@ -251,7 +250,7 @@
     return y * z_size + lax.rem(place_ref[1] + offset, z_size)
 
 
-def merge_part(place, stats, own, maxima, at, bt, groups):
+def merge_part(place, stats, own, maxima, at, bt):
     sources, double, rows = stats.shape
     heads = double // 2
     pairs = heads // 2
@@ -278,10 +277,9 @@
         out_specs=[
             piece_spec,
             piece_spec,
-            pl.BlockSpec((groups, rows, rows), lambda s, place: (0, 0, 0)),
-            pl.BlockSpec((pairs, 8, rows), lambda s, place: (0, 0, 0)),
-        ],
-        scratch_shapes=[pltpu.VMEM((pairs, 8, rows), F32)],
+            pl.BlockSpec((2, heads, rows), lambda s, place: (0, 0, 0)),
+        ],
+        scratch_shapes=[pltpu.VMEM((2, heads, rows), F32)],
     )
     return pl.pallas_call(
         merge_kernel,
@@ -289,10 +287,9 @@
         out_shape=[
             piece,
             piece,
-            jax.ShapeDtypeStruct((groups, rows, rows), F32),
-            jax.ShapeDtypeStruct((pairs, 8, rows), F32),
-        ],
-        compiler_params=pltpu.CompilerParams(vmem_limit_bytes=LIMIT),
+            jax.ShapeDtypeStruct((2, heads, rows), F32),
+        ],
+        compiler_params=pltpu.CompilerParams(vmem_limit_bytes=MERGE_LIMIT),
         cost_estimate=pl.CostEstimate(
             flops=heads * rows * HD, bytes_accessed=3 * 2**20, transcendentals=sources * heads * rows
         ),
@@ -300,56 +297,30 @@
     )(place, stats, own, maxima, at, at, bt, bt)
 
 
-def query_kernel(offset_ref, place_ref, row_ref, at0, at1, bt0, bt1, *out_refs):
+def term_kernel(
+    offset_ref, place_ref, core_ref, all_factor_ref, factor_ref, q_ref, do_ref, e_ref, es_ref,
+    at00, at01, at10, at11, bt00, bt01, bt10, bt11, term_ref, keep_ref, send_ref, row_scr,
+):
     step = pl.program_id(0)
-    pairs = row_ref.shape[0]
-    for slot, at_ref, bt_ref in ((0, at0, bt0), (1, at1, bt1)):
-        pair_rows = row_ref[pair_at(place_ref, offset_ref[step], slot, pairs)]
-        for index, out_ref in enumerate(out_refs):
-
-            @pl.when(step == index)
-            def _(out_ref=out_ref):
-                put_term(out_ref, slot, pair_rows[0:2], pair_rows[2:4], at_ref, bt_ref)
-
-
-def query_part(offsets, place, pair_rows, at, bt):
-    pairs, _, rows = pair_rows.shape
-    count = offsets.shape[0]
-
-    def spec(slot):
-        def index(s, offset, place):
-            return 0, pair_at(place, offset[s], slot, pairs)
-
-        return pl.BlockSpec((HD, 2 * rows), index)
-
-    piece_spec = pl.BlockSpec((2, rows, 2 * HD), lambda s, offset, place: (0, 0, 0))
-    grid_spec = pltpu.PrefetchScalarGridSpec(
-        num_scalar_prefetch=2,
-        grid=(count,),
-        in_specs=[
-            pl.BlockSpec((pairs, 8, rows), lambda s, offset, place: (0, 0, 0)),
-            spec(0), spec(1), spec(0), spec(1),
-        ],
-        out_specs=[piece_spec] * count,
-    )
-    return pl.pallas_call(
-        query_kernel,
-        grid_spec=grid_spec,
-        out_shape=[jax.ShapeDtypeStruct((2, rows, 2 * HD), F32)] * count,
-        compiler_params=pltpu.CompilerParams(vmem_limit_bytes=LIMIT),
-        cost_estimate=pl.CostEstimate(
-            flops=4 * count * 4 * rows * HD, bytes_accessed=5 * 2**20, transcendentals=0
-        ),
-        name="query_terms",
-    )(offsets, place, pair_rows, at, at, bt, bt)
-
-
-def image_kernel(core_ref, factor_ref, q_ref, do_ref, e_ref, es_ref, keep_ref, send_ref):
+    pairs = all_factor_ref.shape[1] // 2
+
+    @pl.when(step == 0)
+    def _():
+        row_scr[...] = all_factor_ref[...] * SCALE
+
+    for i, blocks in enumerate((((at00, bt00), (at01, bt01)), ((at10, bt10), (at11, bt11)))):
+        for slot, (at_ref, bt_ref) in enumerate(blocks):
+            pair = pair_at(place_ref, offset_ref[2 * step + i], slot, pairs)
+            put_term(term_ref.at[i], slot, row_scr, pair, at_ref, bt_ref)
+
     heads = q_ref.shape[1] // HD
+    rows = q_ref.shape[0]
+    fill = jnp.zeros((rows - 2 * heads, rows), F32)
+    columns = jnp.transpose(jnp.concatenate([factor_ref[0], factor_ref[1], fill], axis=0))
     wide_rhs, narrow_rhs = [], []
     for h in range(heads):
-        w = factor_ref[0, :, h : h + 1]
-        wd = factor_ref[0, :, heads + h : heads + h + 1]
+        w = columns[:, h : h + 1]
+        wd = columns[:, heads + h : heads + h + 1]
         q = head(q_ref, h).astype(F32)
         do = head(do_ref, h).astype(F32)
         wide_rhs.append(jnp.concatenate([(w * do).astype(BF16), (wd * q).astype(BF16)], axis=1))
@@ -364,54 +335,59 @@
         for piece in range(pieces):
             even = grad[2 * piece * size : (2 * piece + 1) * size]
             odd = grad[(2 * piece + 1) * size : (2 * piece + 2) * size]
-            keep_ref[piece, :, at : at + HD] = jnp.where(even_core, even, odd)
-            send_ref[piece, :, at : at + HD] = jnp.where(even_core, odd, even)
-
-
-def image_part(core, factors, queries, grad_out, e, es, pieces):
+            y, x = divmod(piece, pieces // 2)
+            x_offset = lax.rem(x + pieces // 2 - core_ref[2], pieces // 2)
+            slot = 2 * x_offset + lax.rem(core_ref[1] + y, 2)
+            keep_ref[slot, :, at : at + HD] = jnp.where(even_core, even, odd)
+            send_ref[slot, :, at : at + HD] = jnp.where(even_core, odd, even)
+
+
+def term_part(order, place, core, factors, queries, grad_out, e, es, at, bt, pieces):
     rows, width = queries.shape
     image_rows, wide = e.shape
-    groups = factors.shape[0]
+    heads = factors.shape[1]
+    pairs = heads // 2
+    groups = heads // 8
     per_group = width // groups
     size = image_rows // (2 * pieces)
-    out = jax.ShapeDtypeStruct((pieces, size, groups * 2 * HD), F32)
-    out_spec = pl.BlockSpec((pieces, size, 2 * HD), lambda g: (0, 0, g))
-    return pl.pallas_call(
-        image_kernel,
+    order = [o % (pairs // 2) for o in order]
+    offsets = jnp.array(order + order[-2:], jnp.int32)
+
+    def spec(i, slot):
+        def index(g, offset, place, core):
+            return 0, pair_at(place, offset[2 * g + i], slot, pairs)
+
+        return pl.BlockSpec((HD, 2 * rows), index)
+
+    four = [spec(i, slot) for i in range(2) for slot in range(2)]
+    half = jax.ShapeDtypeStruct((pieces, size, groups * 2 * HD), F32)
+    half_spec = pl.BlockSpec((pieces, size, 2 * HD), lambda g, *_: (0, 0, g))
+    grid_spec = pltpu.PrefetchScalarGridSpec(
+        num_scalar_prefetch=3,
         grid=(groups,),
         in_specs=[
-            pl.BlockSpec(memory_space=pltpu.SMEM),
-            pl.BlockSpec((1, rows, rows), lambda g: (g, 0, 0)),
-            pl.BlockSpec((rows, per_group), lambda g: (0, g)),
-            pl.BlockSpec((rows, per_group), lambda g: (0, g)),
-            pl.BlockSpec((image_rows, wide // groups), lambda g: (0, g)),
-            pl.BlockSpec((image_rows, wide // groups), lambda g: (0, g)),
-        ],
-        out_specs=[out_spec] * 2,
-        out_shape=[out] * 2,
-        compiler_params=pltpu.CompilerParams(vmem_limit_bytes=LIMIT),
+            pl.BlockSpec((2, heads, rows), lambda g, *_: (0, 0, 0)),
+            pl.BlockSpec((2, heads // groups, rows), lambda g, *_: (0, g, 0)),
+            pl.BlockSpec((rows, per_group), lambda g, *_: (0, g)),
+            pl.BlockSpec((rows, per_group), lambda g, *_: (0, g)),
+            pl.BlockSpec((image_rows, wide // groups), lambda g, *_: (0, g)),
+            pl.BlockSpec((image_rows, wide // groups), lambda g, *_: (0, g)),
+            *four,
+            *four,
+        ],
+        out_specs=[pl.BlockSpec((2, 2, rows, 2 * HD), lambda g, *_: (g, 0, 0, 0)), half_spec, half_spec],
+        scratch_shapes=[pltpu.VMEM((2, heads, rows), F32)],
+    )
+    return pl.pallas_call(
+        term_kernel,
+        grid_spec=grid_spec,
+        out_shape=[jax.ShapeDtypeStruct((2 * groups, 2, rows, 2 * HD), F32), half, half],
+        compiler_params=pltpu.CompilerParams(vmem_limit_bytes=TERM_LIMIT),
         cost_estimate=pl.CostEstimate(
-            flops=6 * width * rows * image_rows, bytes_accessed=15 * 2**20, transcendentals=0
+            flops=6 * width * rows * image_rows, bytes_accessed=20 * 2**20, transcendentals=0
         ),
-        name="image_terms",
-    )(core, factors, queries, grad_out, e, es)
-
-
-def chain(first_right, first_left, later, axis, z_size, y_size):
-    def turn(by):
-        return [
-            (y * z_size + z, y * z_size + (z + by) % z_size) for y in range(y_size) for z in range(z_size)
-        ]
-
-    order = piece_offsets(z_size)[2:]
-    term = dict(zip(order, later))
-    right = lax.ppermute(first_right, axis, turn(1))
-    left = lax.ppermute(first_left, axis, turn(-1))
-    for distance in range(z_size // 2 - 1, 0, -1):
-        right = lax.ppermute(right + term[distance], axis, turn(1))
-        if distance > 1:
-            left = lax.ppermute(left + term[1 - distance], axis, turn(-1))
-    return left, right, term[0]
+        name="query_and_image_terms",
+    )(offsets, place, core, factors, factors, queries, grad_out, e, es, *[at] * 4, *[bt] * 4)
 
 
 def on_device(queries, keys, values, grad_out, keep_blocks):
@@ -421,30 +397,68 @@
     z_size = image_size // y_size
     pieces = text_size // 2
     groups = keys.shape[1] // HD
-    core_groups = [[2 * k + c for k in range(pieces)] for c in range(2)]
-    swap_y = [(i, (i + z_size) % image_size) for i in range(image_size)]
+    swap_far = [(t, (t + pieces) % text_size) for t in range(text_size)]
     swap_core = [(t, t ^ 1) for t in range(text_size)]
     image_index = lax.axis_index("image").astype(jnp.int32)
     place = jnp.stack([image_index // z_size, image_index % z_size])
-    offsets = jnp.array([o % z_size for o in piece_offsets(z_size)[2:]], jnp.int32)
-    core = (lax.axis_index("text") % 2).astype(jnp.int32).reshape(1)
+    text_index = lax.axis_index("text").astype(jnp.int32)
+    x_size = pieces // 2
+    core = jnp.stack([text_index % 2, text_index // pieces, text_index // 2 % x_size])
+
+    def turn_x(by):
+        return [
+            (y * pieces + 2 * x + c, y * pieces + (2 * x + 2 * by) % pieces + c)
+            for y in range(2)
+            for x in range(x_size)
+            for c in range(2)
+        ]
+
+    def turn(by, across=0):
+        return [
+            (y * z_size + z, (y + across) % y_size * z_size + (z + by) % z_size)
+            for y in range(y_size)
+            for z in range(z_size)
+        ]
 
     e, own, maxima = local_part(keep_blocks, queries, grad_out, keys, values, image_size)
     stats = lax.all_to_all(own, "image", 0, 0, tiled=True)
     es, at, bt = product_part(own, grad_out, keys, values, e)
-    first_right, first_left, factors, pair_rows = merge_part(place, stats, own, maxima, at, bt, groups)
-    later = query_part(offsets, place, pair_rows, at, bt)
-    left, right, here = chain(first_right, first_left, later, "image", z_size, y_size)
-    query_sum = left + right + here
-    grad_queries = (query_sum[0] + lax.ppermute(query_sum[1], "image", swap_y)).astype(BF16)
-
-    keep, send = image_part(core, factors, queries, grad_out, e, es, pieces)
-    image_terms = keep + lax.ppermute(send, "text", swap_core)
-    text_arrived = lax.all_to_all(image_terms, "text", 0, 0, tiled=True, axis_index_groups=core_groups)
-    image_sum = jnp.sum(text_arrived, axis=0)
-    both = image_sum.reshape(image_sum.shape[0], groups, 2, HD)
-    grad_keys = both[:, :, 0].reshape(-1, groups * HD).astype(BF16)
-    grad_values = both[:, :, 1].reshape(-1, groups * HD).astype(BF16)
+
+    first_right, first_left, factors = merge_part(place, stats, own, maxima, at, bt)
+    right = lax.ppermute(first_right, "image", turn(1))
+    left = lax.ppermute(first_left, "image", turn(-1))
+    order = piece_offsets(z_size)[2:]
+    terms, keep, send = term_part(
+        order, place, core, factors, queries, grad_out, e, es, at, bt, pieces
+    )
+    terms, keep, send, right, left = lax.optimization_barrier((terms, keep, send, right, left))
+    term = {offset: terms[i] for i, offset in enumerate(order)}
+    received = lax.ppermute(send, "text", swap_core)
+    right = lax.ppermute(right + term[3], "image", turn(1))
+    left = lax.ppermute(left + term[-2], "image", turn(-1))
+    image_terms = keep + received
+    part = [image_terms[2 * by : 2 * by + 2] for by in range(x_size)]
+    x_right = lax.ppermute(part[2][0], "text", turn_x(1))
+    x_left = lax.ppermute(part[2][1], "text", turn_x(-1))
+    right, left, x_right, x_left = lax.optimization_barrier((right, left, x_right, x_left))
+    right = lax.ppermute(right + term[2], "image", turn(1))
+    left = lax.ppermute(left + term[-1], "image", turn(-1))
+    x_right = lax.ppermute(jnp.stack([part[1][0] + x_right, part[1][1]]), "text", turn_x(1))
+    x_left = lax.ppermute(jnp.stack([part[3][0], part[3][1] + x_left]), "text", turn_x(-1))
+    right, left = lax.optimization_barrier((right, left))
+    x_sum = part[0] + x_right + x_left
+    image_sum = x_sum[0] + lax.ppermute(x_sum[1], "text", swap_far)
+    over = right + term[1]
+    here = left + term[0]
+    query_sum = (
+        here[0]
+        + lax.ppermute(over[0], "image", turn(1))
+        + lax.ppermute(over[1], "image", turn(1, 1))
+        + lax.ppermute(here[1], "image", turn(0, 1))
+    )
+    grad_queries = query_sum.astype(BF16)
+    grad_keys = jnp.concatenate([head(image_sum, 2 * g) for g in range(groups)], axis=1).astype(BF16)
+    grad_values = jnp.concatenate([head(image_sum, 2 * g + 1) for g in range(groups)], axis=1).astype(BF16)
     return (grad_queries, grad_keys, grad_values)
 
 

time: 96.3 us -> 89 us (0.924); the launches traced: 94.6 us -> 88.6 us
  Pallas kernels: 34.9 us -> 30.6 us
  starting transfers between devices: 28.3 us -> 27 us
  waiting for transfers between devices: 23.7 us -> 25 us
  local copies, waits for them, and re-layouts: 1.98 us -> 0.91 us
    all_to_all x1 -> x0, starting transfers between devices: 6.16 us -> none  [on_device(): lax.all_to_all(image_terms, 'text', 0, 0, tiled=True, axis_index_groups=c...]
    ppermute x9 -> x15, starting transfers between devices: 12.2 us -> 17.1 us  [the longest x1 2.84 us: on_device(): x_left = lax.ppermute(part[2][1], 'text', turn_x(-1))]
    pallas_call x2 -> x1, Pallas kernels: 14.8 us -> 10.5 us  [term_part(): pl.pallas_call(term_kernel, grid_spec=grid_spec, out_shape=[jax.ShapeDtyp...]
    add x7 -> x5, other arithmetic: 3.6 us -> 1.62 us  [the longest x1 1.18 us: on_device(): left = lax.ppermute(left + term[-2], 'image', turn(-1))]
    ppermute x9 -> x15, waiting for transfers between devices: 18.7 us -> 20.2 us  [the longest x1 3.44 us: on_device(): left = lax.ppermute(left + term[-2], 'image', turn(-1))]
  transfers between devices with their start and end apart: 11 -> 16, of which waited for: 6 -> 11; matrix products, arithmetic and copies ran while one was open for 5% -> 4% of each run, Pallas kernels for 16% -> 22%
where the time goes in v3:
time: 89 us; the launch traced here: 88.6 us
  Pallas kernels  30.6 us (34%)
  starting transfers between devices  27 us (30%)
  waiting for transfers between devices  25 us (28%)
  other arithmetic  4.28 us (5%)
  local copies, waits for them, and re-layouts  0.91 us (1%)
    pallas_call x1, Pallas kernels, term_part(): pl.pallas_call(term_kernel, grid_spec=grid_spec, out_shape=[jax.ShapeDtyp...  10.5 us
    all_to_all x1, starting transfers between devices, on_device(): stats = lax.all_to_all(own, 'image', 0, 0, tiled=True)  9.96 us
    pallas_call x1, Pallas kernels, product_part(): pl.pallas_call(product_kernel, grid=(groups,), in_specs=[pl.BlockSpec((1,...  8.96 us
    pallas_call x1, Pallas kernels, local_part(): pl.pallas_call(local_kernel, grid=(groups,), in_specs=[pl.BlockSpec(memor...  7.57 us
    all_to_all x1, waiting for transfers between devices, on_device(): stats = lax.all_to_all(own, 'image', 0, 0, tiled=True)  4.84 us
    pallas_call x1, Pallas kernels, merge_part(): pl.pallas_call(merge_kernel, grid_spec=grid_spec, out_shape=[piece, piece...  3.49 us
    ppermute x1, waiting for transfers between devices, on_device(): left = lax.ppermute(left + term[-2], 'image', turn(-1))  3.44 us
    ppermute x1, waiting for transfers between devices, on_device(): right = lax.ppermute(right + term[2], 'image', turn(1))  3.09 us
  transfers between devices with their start and end apart: 16, of which 11 were waited for; matrix products, arithmetic and copies ran while one was open for 4% of the time, Pallas kernels for 22%

profile of v3, /device:TPU:8, one launch (start us, length us, event | category | flops | bytes accessed | tf_op | source)
XLA Modules:
  0.0 88.6 jit_solution(4495985901731413446)
XLA Ops:
  0.6 7.6 %local_statistics.1 = (bf16[640,4096]{1,0:T(8,128)(2,1)}, f32[16,64,128]{2,1,0:T(8,128)}, f32[32,128]{1,0:T(8,128)}) custom-call(s32[2,5]{1,0:T(2,128)} %keep_ref.1, bf16[128,4096]{1,0:T(8,128)(2,1)} %q_ref.3, bf16[128,4096]{1,0:T(8,128)(2,1)} %do_ref.5, bf16[640,512]{1,0:T(8,128)(2,1)} %k_ref.3, bf16[640,512]{1,0:T(8,128)(2,1)} %v_ref.3), custom_call_target="tpu_custom_call" | custom-call | flops 1342177280 | bytes 9437184 | tf_op jit(solution)/shard_map/local_statistics/pallas_call | solution.py:105
  8.2 10.0 %all-to-all-start = ((f32[16,64,128]{2,1,0:T(8,128)}), f32[16,64,128]{2,1,0:T(8,128)S(1)}, u32[]{:S(2)}, u32[]{:S(2)}) async-start(f32[16,64,128]{2,1,0:T(8,128)} %get-tuple-element.26.own_ref), calls=%async_computation | async-start | bytes 1048576 | tf_op jit(solution)/shard_map/all_to_all | solution.py:424
  18.8 9.0 %local_products.1 = (bf16[640,4096]{1,0:T(8,128)(2,1)}, f32[128,4096]{1,0:T(8,128)}, f32[128,4096]{1,0:T(8,128)}) custom-call(f32[16,64,128]{2,1,0:T(8,128)} %get-tuple-element.26.own_ref, bf16[128,4096]{1,0:T(8,128)(2,1)} %do_ref.5, bf16[640,512]{1,0:T(8,128)(2,1)} %k_ref.3, bf16[640,512]{1,0:T(8,128)(2,1)} %v_ref.3, bf16[640,4096]{1,0:T(8,128)(2,1)} %get-tuple-element.28.e_ref), custom_call_target="tpu_custom_call" | custom-call | flops 2013265920 | bytes 18874368 | tf_op jit(solution)/shard_map/local_products/pallas_call | solution.py:164
  27.8 4.8 %all-to-all-done.all_ref = f32[16,64,128]{2,1,0:T(8,128)S(1)} async-done(((f32[16,64,128]{2,1,0:T(8,128)}), f32[16,64,128]{2,1,0:T(8,128)S(1)}, u32[]{:S(2)}, u32[]{:S(2)}) %all-to-all-start) | async-done | bytes 524320 | tf_op jit(solution)/shard_map/all_to_all | solution.py:424
  33.4 3.5 %merged_statistics.1 = (f32[2,128,256]{2,1,0:T(8,128)}, f32[2,128,256]{2,1,0:T(8,128)}, f32[2,32,128]{2,1,0:T(8,128)}) custom-call(s32[2]{0:T(128)} %pad_add_fusion.place_ref, f32[16,64,128]{2,1,0:T(8,128)} %copy-done, f32[16,64,128]{2,1,0:T(8,128)} %get-tuple-element.26.own_ref, f32[32,128]{1,0:T(8,128)} %get-tuple-element.27.max_ref, ...), custom_call_target="tpu_custom_call" | custom-call | flops 524288 | bytes 3145728 | tf_op jit(solution)/shard_map/merged_statistics/pallas_call | solution.py:284
  36.9 2.1 %collective-permute-start = (f32[2,128,256]{2,1,0:T(8,128)}, f32[2,128,256]{2,1,0:T(8,128)S(1)}, u32[]{:S(2)}, u32[]{:S(2)}) collective-permute-start(f32[2,128,256]{2,1,0:T(8,128)} %get-tuple-element.36), channel_id=1, source_target_pairs={{0,1},{1,2},{2,3},{3,4},{4,5},{5,6},{6,7},{7,0},{8,9},{9,10},{10,1... | collective-permute-start | bytes 786440 | tf_op jit(solution)/shard_map/ppermute | solution.py:428
  40.7 10.5 %query_and_image_terms.1 = (f32[8,2,128,256]{3,2,1,0:T(8,128)}, f32[8,40,1024]{2,1,0:T(8,128)}, f32[8,40,1024]{2,1,0:T(8,128)}) custom-call(s32[8]{0:T(128)} %constant.68.clone.offset_ref, s32[2]{0:T(128)} %pad_add_fusion.place_ref, s32[3]{0:T(128)} %pad_add_fusion.1.core_ref, f32[2,32,128]{2,1,0:T(8,128)} %get-tuple-element.31.all_factor_ref.factor_ref, ...), custom_call_target="tpu_custom_call" | custom-call | flops 2013265920 | bytes 20971520 | tf_op jit(solution)/shard_map/query_and_image_terms/pallas_call | solution.py:381
  51.4 1.2 %bitcast_add_fusion.4 = (f32[2,128,256]{2,1,0:T(8,128)S(1)}, f32[2,128,256]{2,1,0:T(8,128)S(1)}) fusion(f32[2,128,256]{2,1,0:T(8,128)S(1)} %collective-permute-done.1, f32[8,2,128,256]{3,2,1,0:T(8,128)} %get-tuple-element.39, f32[2,128,256]{2,1,0:T(8,128)S(1)} %collective-permute-done), kind=kLoop, calls=%fused_computation.8 | loop fusion | flops 131072 | bytes 1572864 | tf_op jit(solution)/shard_map/add | solution.py:438
  52.6 1.5 %collective-permute-start.3 = (f32[2,128,256]{2,1,0:T(8,128)S(1)}, f32[2,128,256]{2,1,0:T(8,128)S(1)}, u32[]{:S(2)}, u32[]{:S(2)}) collective-permute-start(f32[2,128,256]{2,1,0:T(8,128)S(1)} %get-tuple-element.53), channel_id=1, source_target_pairs={{0,7},{1,0},{2,1},{3,2},{4,3},{5,4},{6,5},{7,6},{8,15},{9,8},{10,9... | collective-permute-start | bytes 786440 | tf_op jit(solution)/shard_map/ppermute | solution.py:438
  55.0 2.8 %collective-permute-start.6 = (f32[40,1024]{1,0:T(8,128)S(1)}, f32[40,1024]{1,0:T(8,128)S(1)}, u32[]{:S(2)}, u32[]{:S(2)}) collective-permute-start(f32[40,1024]{1,0:T(8,128)S(1)} %get-tuple-element.59), channel_id=1, source_target_pairs={{0,96},{16,112},{32,0},{48,16},{64,32},{80,48},{96,64},{112,80},{1... | collective-permute-start | bytes 491528 | tf_op jit(solution)/shard_map/ppermute | solution.py:442
  57.9 3.4 %collective-permute-done.3 = f32[2,128,256]{2,1,0:T(8,128)S(1)} collective-permute-done((f32[2,128,256]{2,1,0:T(8,128)S(1)}, f32[2,128,256]{2,1,0:T(8,128)S(1)}, u32[]{:S(2)}, u32[]{:S(2)}) %collective-permute-start.3) | collective-permute-done | bytes 262176 | tf_op jit(solution)/shard_map/ppermute | solution.py:438
  61.3 2.3 %collective-permute-done.2 = f32[2,128,256]{2,1,0:T(8,128)S(1)} collective-permute-done((f32[2,128,256]{2,1,0:T(8,128)S(1)}, f32[2,128,256]{2,1,0:T(8,128)S(1)}, u32[]{:S(2)}, u32[]{:S(2)}) %collective-permute-start.2) | collective-permute-done | bytes 262176 | tf_op jit(solution)/shard_map/ppermute | solution.py:437
  63.6 1.3 %collective-permute-done.5 = f32[40,1024]{1,0:T(8,128)S(1)} collective-permute-done((f32[40,1024]{1,0:T(8,128)S(1)}, f32[40,1024]{1,0:T(8,128)S(1)}, u32[]{:S(2)}, u32[]{:S(2)}) %collective-permute-start.5) | collective-permute-done | bytes 163872 | tf_op jit(solution)/shard_map/ppermute | solution.py:441
  65.1 2.5 %collective-permute-start.8 = (f32[2,128,256]{2,1,0:T(8,128)S(1)}, f32[2,128,256]{2,1,0:T(8,128)S(1)}, u32[]{:S(2)}, u32[]{:S(2)}) collective-permute-start(f32[2,128,256]{2,1,0:T(8,128)S(1)} %get-tuple-element.51), channel_id=1, source_target_pairs={{0,7},{1,0},{2,1},{3,2},{4,3},{5,4},{6,5},{7,6},{8,15},{9,8},{10,9... | collective-permute-start | bytes 786440 | tf_op jit(solution)/shard_map/ppermute | solution.py:445
  67.6 1.1 %collective-permute-start.13 = (f32[2,40,1024]{2,1,0:T(8,128)S(1)}, f32[2,40,1024]{2,1,0:T(8,128)S(1)}, u32[]{:S(2)}, u32[]{:S(2)}) collective-permute-start(f32[2,40,1024]{2,1,0:T(8,128)S(1)} %pad_maximum_fusion.1), channel_id=1, source_target_pairs={{0,96},{16,112},{32,0},{48,16},{64,32},{80,48},{96,64},{112,80},{1... | collective-permute-start | bytes 983048 | tf_op jit(solution)/shard_map/ppermute | solution.py:447
  68.8 1.2 %collective-permute-start.12 = (f32[2,40,1024]{2,1,0:T(8,128)S(1)}, f32[2,40,1024]{2,1,0:T(8,128)S(1)}, u32[]{:S(2)}, u32[]{:S(2)}) collective-permute-start(f32[2,40,1024]{2,1,0:T(8,128)S(1)} %pad_maximum_fusion), channel_id=1, source_target_pairs={{0,32},{16,48},{32,64},{48,80},{64,96},{80,112},{96,0},{112,16},{1... | collective-permute-start | bytes 983048 | tf_op jit(solution)/shard_map/ppermute | solution.py:446
  70.0 2.3 %collective-permute-done.8 = f32[2,128,256]{2,1,0:T(8,128)S(1)} collective-permute-done((f32[2,128,256]{2,1,0:T(8,128)S(1)}, f32[2,128,256]{2,1,0:T(8,128)S(1)}, u32[]{:S(2)}, u32[]{:S(2)}) %collective-permute-start.8) | collective-permute-done | bytes 262176 | tf_op jit(solution)/shard_map/ppermute | solution.py:445
  72.3 3.1 %collective-permute-done.7 = f32[2,128,256]{2,1,0:T(8,128)S(1)} collective-permute-done((f32[2,128,256]{2,1,0:T(8,128)S(1)}, f32[2,128,256]{2,1,0:T(8,128)S(1)}, u32[]{:S(2)}, u32[]{:S(2)}) %collective-permute-start.7) | collective-permute-done | bytes 262176 | tf_op jit(solution)/shard_map/ppermute | solution.py:444
  75.4 1.4 %collective-permute-start.11 = (f32[128,256]{1,0:T(8,128)S(1)}, f32[128,256]{1,0:T(8,128)S(1)}, u32[]{:S(2)}, u32[]{:S(2)}) collective-permute-start(f32[128,256]{1,0:T(8,128)S(1)} %slice_bitcast_fusion.6), channel_id=1, source_target_pairs={{0,8},{1,9},{2,10},{3,11},{4,12},{5,13},{6,14},{7,15},{8,0},{9,1},... | collective-permute-start | bytes 393224 | tf_op jit(solution)/shard_map/ppermute | solution.py:457
  77.0 1.3 %collective-permute-done.12 = f32[2,40,1024]{2,1,0:T(8,128)S(1)} collective-permute-done((f32[2,40,1024]{2,1,0:T(8,128)S(1)}, f32[2,40,1024]{2,1,0:T(8,128)S(1)}, u32[]{:S(2)}, u32[]{:S(2)}) %collective-permute-start.12) | collective-permute-done | bytes 327712 | tf_op jit(solution)/shard_map/ppermute | solution.py:446
  78.4 2.4 %collective-permute-start.14 = (f32[40,1024]{1,0:T(8,128)S(1)}, f32[40,1024]{1,0:T(8,128)S(1)}, u32[]{:S(2)}, u32[]{:S(2)}) collective-permute-start(f32[40,1024]{1,0:T(8,128)S(1)} %slice_bitcast_fusion), channel_id=1, source_target_pairs={{0,128},{16,144},{32,160},{48,176},{64,192},{80,208},{96,224},{112... | collective-permute-start | bytes 491528 | tf_op jit(solution)/shard_map/ppermute | solution.py:450
  80.8 1.9 %collective-permute-done.11 = f32[128,256]{1,0:T(8,128)S(1)} collective-permute-done((f32[128,256]{1,0:T(8,128)S(1)}, f32[128,256]{1,0:T(8,128)S(1)}, u32[]{:S(2)}, u32[]{:S(2)}) %collective-permute-start.11) | collective-permute-done | bytes 131104 | tf_op jit(solution)/shard_map/ppermute | solution.py:457
  83.1 1.7 %collective-permute-done.10 = f32[128,256]{1,0:T(8,128)S(1)} collective-permute-done((f32[128,256]{1,0:T(8,128)S(1)}, f32[128,256]{1,0:T(8,128)S(1)}, u32[]{:S(2)}, u32[]{:S(2)}) %collective-permute-start.10) | collective-permute-done | bytes 131104 | tf_op jit(solution)/shard_map/ppermute | solution.py:456
  85.4 2.4 %collective-permute-done.14 = f32[40,1024]{1,0:T(8,128)S(1)} collective-permute-done((f32[40,1024]{1,0:T(8,128)S(1)}, f32[40,1024]{1,0:T(8,128)S(1)}, u32[]{:S(2)}, u32[]{:S(2)}) %collective-permute-start.14) | collective-permute-done | bytes 163872 | tf_op jit(solution)/shard_map/ppermute | solution.py:450
  (36 shorter events, 6.4 us)
Async XLA Ops:
  8.2 24.4 %all-to-all-start = ((f32[16,64,128]{2,1,0:T(8,128)}), f32[16,64,128]{2,1,0:T(8,128)S(1)}, u32[]{:S(2)}, u32[]{:S(2)}) async-start(f32[16,64,128]{2,1,0:T(8,128)} %get-tuple-element.26.own_ref), calls=%async_computation | async-start | bytes 1048576 | tf_op jit(solution)/shard_map/all_to_all | solution.py:424
  32.6 0.8 copy-start
  36.9 14.4 %collective-permute-start = (f32[2,128,256]{2,1,0:T(8,128)}, f32[2,128,256]{2,1,0:T(8,128)S(1)}, u32[]{:S(2)}, u32[]{:S(2)}) collective-permute-start(f32[2,128,256]{2,1,0:T(8,128)} %get-tuple-element.36), channel_id=1, source_target_pairs={{0,1},{1,2},{2,3},{3,4},{4,5},{5,6},{6,7},{7,0},{8,9},{9,10},{10,1... | collective-permute-start | bytes 786440 | tf_op jit(solution)/shard_map/ppermute | solution.py:428
  39.0 12.3 %collective-permute-start.1 = (f32[2,128,256]{2,1,0:T(8,128)}, f32[2,128,256]{2,1,0:T(8,128)S(1)}, u32[]{:S(2)}, u32[]{:S(2)}) collective-permute-start(f32[2,128,256]{2,1,0:T(8,128)} %get-tuple-element.37), channel_id=1, source_target_pairs={{0,7},{1,0},{2,1},{3,2},{4,3},{5,4},{6,5},{7,6},{8,15},{9,8},{10,9... | collective-permute-start | bytes 786440 | tf_op jit(solution)/shard_map/ppermute | solution.py:429
  51.3 3.4 %copy-start.1 = (f32[8,40,1024]{2,1,0:T(8,128)S(1)}, f32[8,40,1024]{2,1,0:T(8,128)}, u32[]{:S(2)}) copy-start(f32[8,40,1024]{2,1,0:T(8,128)} %get-tuple-element.41) | copy-start | bytes 3932164
  51.3 3.4 %collective-permute-start.4 = (f32[8,40,1024]{2,1,0:T(8,128)}, f32[8,40,1024]{2,1,0:T(8,128)S(1)}, u32[]{:S(2)}, u32[]{:S(2)}) collective-permute-start(f32[8,40,1024]{2,1,0:T(8,128)} %get-tuple-element.42), channel_id=1, source_target_pairs={{0,16},{16,0},{32,48},{48,32},{64,80},{80,64},{96,112},{112,96},{1... | collective-permute-start | bytes 3932168 | tf_op jit(solution)/shard_map/ppermute | solution.py:436
  52.6 8.7 %collective-permute-start.3 = (f32[2,128,256]{2,1,0:T(8,128)S(1)}, f32[2,128,256]{2,1,0:T(8,128)S(1)}, u32[]{:S(2)}, u32[]{:S(2)}) collective-permute-start(f32[2,128,256]{2,1,0:T(8,128)S(1)} %get-tuple-element.53), channel_id=1, source_target_pairs={{0,7},{1,0},{2,1},{3,2},{4,3},{5,4},{6,5},{7,6},{8,15},{9,8},{10,9... | collective-permute-start | bytes 786440 | tf_op jit(solution)/shard_map/ppermute | solution.py:438
  54.1 10.9 %copy-start.2 = (f32[8,2,128,256]{3,2,1,0:T(8,128)S(1)}, f32[8,2,128,256]{3,2,1,0:T(8,128)}, u32[]{:S(2)}) copy-start(f32[8,2,128,256]{3,2,1,0:T(8,128)} %get-tuple-element.39) | copy-start | bytes 6291460
  54.1 9.6 %collective-permute-start.2 = (f32[2,128,256]{2,1,0:T(8,128)S(1)}, f32[2,128,256]{2,1,0:T(8,128)S(1)}, u32[]{:S(2)}, u32[]{:S(2)}) collective-permute-start(f32[2,128,256]{2,1,0:T(8,128)S(1)} %get-tuple-element.54), channel_id=1, source_target_pairs={{0,1},{1,2},{2,3},{3,4},{4,5},{5,6},{6,7},{7,0},{8,9},{9,10},{10,1... | collective-permute-start | bytes 786440 | tf_op jit(solution)/shard_map/ppermute | solution.py:437
  55.0 8.6 %collective-permute-start.6 = (f32[40,1024]{1,0:T(8,128)S(1)}, f32[40,1024]{1,0:T(8,128)S(1)}, u32[]{:S(2)}, u32[]{:S(2)}) collective-permute-start(f32[40,1024]{1,0:T(8,128)S(1)} %get-tuple-element.59), channel_id=1, source_target_pairs={{0,96},{16,112},{32,0},{48,16},{64,32},{80,48},{96,64},{112,80},{1... | collective-permute-start | bytes 491528 | tf_op jit(solution)/shard_map/ppermute | solution.py:442
  57.9 7.1 %collective-permute-start.5 = (f32[40,1024]{1,0:T(8,128)S(1)}, f32[40,1024]{1,0:T(8,128)S(1)}, u32[]{:S(2)}, u32[]{:S(2)}) collective-permute-start(f32[40,1024]{1,0:T(8,128)S(1)} %get-tuple-element.60), channel_id=1, source_target_pairs={{0,32},{16,48},{32,64},{48,80},{64,96},{80,112},{96,0},{112,16},{1... | collective-permute-start | bytes 491528 | tf_op jit(solution)/shard_map/ppermute | solution.py:441
  65.1 7.2 %collective-permute-start.8 = (f32[2,128,256]{2,1,0:T(8,128)S(1)}, f32[2,128,256]{2,1,0:T(8,128)S(1)}, u32[]{:S(2)}, u32[]{:S(2)}) collective-permute-start(f32[2,128,256]{2,1,0:T(8,128)S(1)} %get-tuple-element.51), channel_id=1, source_target_pairs={{0,7},{1,0},{2,1},{3,2},{4,3},{5,4},{6,5},{7,6},{8,15},{9,8},{10,9... | collective-permute-start | bytes 786440 | tf_op jit(solution)/shard_map/ppermute | solution.py:445
  67.5 7.8 %collective-permute-start.7 = (f32[2,128,256]{2,1,0:T(8,128)S(1)}, f32[2,128,256]{2,1,0:T(8,128)S(1)}, u32[]{:S(2)}, u32[]{:S(2)}) collective-permute-start(f32[2,128,256]{2,1,0:T(8,128)S(1)} %get-tuple-element.52), channel_id=1, source_target_pairs={{0,1},{1,2},{2,3},{3,4},{4,5},{5,6},{6,7},{7,0},{8,9},{9,10},{10,1... | collective-permute-start | bytes 786440 | tf_op jit(solution)/shard_map/ppermute | solution.py:444
  67.6 9.4 %collective-permute-start.13 = (f32[2,40,1024]{2,1,0:T(8,128)S(1)}, f32[2,40,1024]{2,1,0:T(8,128)S(1)}, u32[]{:S(2)}, u32[]{:S(2)}) collective-permute-start(f32[2,40,1024]{2,1,0:T(8,128)S(1)} %pad_maximum_fusion.1), channel_id=1, source_target_pairs={{0,96},{16,112},{32,0},{48,16},{64,32},{80,48},{96,64},{112,80},{1... | collective-permute-start | bytes 983048 | tf_op jit(solution)/shard_map/ppermute | solution.py:447
  68.8 9.6 %collective-permute-start.12 = (f32[2,40,1024]{2,1,0:T(8,128)S(1)}, f32[2,40,1024]{2,1,0:T(8,128)S(1)}, u32[]{:S(2)}, u32[]{:S(2)}) collective-permute-start(f32[2,40,1024]{2,1,0:T(8,128)S(1)} %pad_maximum_fusion), channel_id=1, source_target_pairs={{0,32},{16,48},{32,64},{48,80},{64,96},{80,112},{96,0},{112,16},{1... | collective-permute-start | bytes 983048 | tf_op jit(solution)/shard_map/ppermute | solution.py:446
  75.4 7.3 %collective-permute-start.11 = (f32[128,256]{1,0:T(8,128)S(1)}, f32[128,256]{1,0:T(8,128)S(1)}, u32[]{:S(2)}, u32[]{:S(2)}) collective-permute-start(f32[128,256]{1,0:T(8,128)S(1)} %slice_bitcast_fusion.6), channel_id=1, source_target_pairs={{0,8},{1,9},{2,10},{3,11},{4,12},{5,13},{6,14},{7,15},{8,0},{9,1},... | collective-permute-start | bytes 393224 | tf_op jit(solution)/shard_map/ppermute | solution.py:457
  76.9 6.3 %collective-permute-start.9 = (f32[128,256]{1,0:T(8,128)S(1)}, f32[128,256]{1,0:T(8,128)S(1)}, u32[]{:S(2)}, u32[]{:S(2)}) collective-permute-start(f32[128,256]{1,0:T(8,128)S(1)} %get-tuple-element.61), channel_id=1, source_target_pairs={{0,1},{1,2},{2,3},{3,4},{4,5},{5,6},{6,7},{7,0},{8,9},{9,10},{10,1... | collective-permute-start | bytes 393224 | tf_op jit(solution)/shard_map/ppermute | solution.py:455
  76.9 7.8 %collective-permute-start.10 = (f32[128,256]{1,0:T(8,128)S(1)}, f32[128,256]{1,0:T(8,128)S(1)}, u32[]{:S(2)}, u32[]{:S(2)}) collective-permute-start(f32[128,256]{1,0:T(8,128)S(1)} %get-tuple-element.62), channel_id=1, source_target_pairs={{0,9},{1,10},{2,11},{3,12},{4,13},{5,14},{6,15},{7,8},{8,1},{9,2},... | collective-permute-start | bytes 393224 | tf_op jit(solution)/shard_map/ppermute | solution.py:456
  78.4 9.5 %collective-permute-start.14 = (f32[40,1024]{1,0:T(8,128)S(1)}, f32[40,1024]{1,0:T(8,128)S(1)}, u32[]{:S(2)}, u32[]{:S(2)}) collective-permute-start(f32[40,1024]{1,0:T(8,128)S(1)} %slice_bitcast_fusion), channel_id=1, source_target_pairs={{0,128},{16,144},{32,160},{48,176},{64,192},{80,208},{96,224},{112... | collective-permute-start | bytes 491528 | tf_op jit(solution)/shard_map/ppermute | solution.py:450

commit v4 on v3

--- a/solution.py
+++ b/solution.py
@@ -205,43 +205,35 @@
 
 
 def merge_kernel(
-    place_ref, all_ref, own_ref, max_ref, at0, at1, bt0, bt1, right_ref, left_ref, factor_ref, row_scr
+    place_ref, all_ref, own_ref, max_ref, at00, at01, at10, at11, bt00, bt01, bt10, bt11,
+    right_ref, left_ref, factor_ref, row_scr,
 ):
-    step = pl.program_id(0)
     sources, double, rows = all_ref.shape
     heads = double // 2
     pairs = heads // 2
 
-    @pl.when(step == 0)
-    def _():
-        logs = [all_ref[s, 0:heads, :] for s in range(sources)]
-        top = logs[0]
-        for log in logs[1:]:
-            top = jnp.maximum(top, log)
-        total = jnp.zeros((heads, rows), F32)
-        product = jnp.zeros((heads, rows), F32)
-        for s in range(sources):
-            share = jnp.exp(logs[s] - top)
-            total = total + share
-            product = product + share * all_ref[s, heads:double, :]
-        w = jnp.exp(max_ref[...] - (top + jnp.log(total)))
-        d = w * (own_ref[0, heads:double, :] - product / total)
-        factor_ref[0] = w
-        factor_ref[1] = d
-        row_scr[0] = w * SCALE
-        row_scr[1] = d * SCALE
-
-    offset = jnp.where(step == 0, pairs // 4, pairs // 2 - pairs // 4 + 1)
-    for slot, at_ref, bt_ref in ((0, at0, bt0), (1, at1, bt1)):
-        pair = pair_at(place_ref, offset, slot, pairs)
-
-        @pl.when(step == 0)
-        def _():
-            put_term(right_ref, slot, row_scr, pair, at_ref, bt_ref)
-
-        @pl.when(step == 1)
-        def _():
-            put_term(left_ref, slot, row_scr, pair, at_ref, bt_ref)
+    logs = [all_ref[s, 0:heads, :] for s in range(sources)]
+    top = logs[0]
+    for log in logs[1:]:
+        top = jnp.maximum(top, log)
+    total = jnp.zeros((heads, rows), F32)
+    product = jnp.zeros((heads, rows), F32)
+    for s in range(sources):
+        share = jnp.exp(logs[s] - top)
+        total = total + share
+        product = product + share * all_ref[s, heads:double, :]
+    w = jnp.exp(max_ref[...] - (top + jnp.log(total)))
+    d = w * (own_ref[0, heads:double, :] - product / total)
+    factor_ref[0] = w
+    factor_ref[1] = d
+    row_scr[0] = w * SCALE
+    row_scr[1] = d * SCALE
+    z_size = pairs // 2
+    first, second = (o % z_size for o in piece_offsets(z_size)[:2])
+    for slot, at_ref, bt_ref in ((0, at00, bt00), (1, at01, bt01)):
+        put_term(right_ref, slot, row_scr, pair_at(place_ref, first, slot, pairs), at_ref, bt_ref)
+    for slot, at_ref, bt_ref in ((0, at10, bt10), (1, at11, bt11)):
+        put_term(left_ref, slot, row_scr, pair_at(place_ref, second, slot, pairs), at_ref, bt_ref)
 
 
 def pair_at(place_ref, offset, slot, pairs):
@@ -255,24 +247,26 @@
     heads = double // 2
     pairs = heads // 2
     z_size = pairs // 2
-    first, second = (o % z_size for o in piece_offsets(z_size)[:2])
-
-    def spec(slot):
-        def index(s, place):
-            return 0, pair_at(place, jnp.where(s == 0, first, second), slot, pairs)
-
-        return pl.BlockSpec((HD, 2 * rows), index)
-
+
+    def spec(offset, slot):
+        return pl.BlockSpec(
+            (HD, 2 * rows), lambda s, place: (0, pair_at(place, offset, slot, pairs))
+        )
+
+    four = [
+        spec(offset % z_size, slot) for offset in piece_offsets(z_size)[:2] for slot in range(2)
+    ]
     piece = jax.ShapeDtypeStruct((2, rows, 2 * HD), F32)
     piece_spec = pl.BlockSpec((2, rows, 2 * HD), lambda s, place: (0, 0, 0))
     grid_spec = pltpu.PrefetchScalarGridSpec(
         num_scalar_prefetch=1,
-        grid=(2,),
+        grid=(1,),
         in_specs=[
             pl.BlockSpec((sources, double, rows), lambda s, place: (0, 0, 0)),
             pl.BlockSpec((1, double, rows), lambda s, place: (0, 0, 0)),
             pl.BlockSpec((heads, rows), lambda s, place: (0, 0)),
-            spec(0), spec(1), spec(0), spec(1),
+            *four,
+            *four,
         ],
         out_specs=[
             piece_spec,
@@ -294,11 +288,11 @@
             flops=heads * rows * HD, bytes_accessed=3 * 2**20, transcendentals=sources * heads * rows
         ),
         name="merged_statistics",
-    )(place, stats, own, maxima, at, at, bt, bt)
+    )(place, stats, own, maxima, *[at] * 4, *[bt] * 4)
 
 
 def term_kernel(
-    offset_ref, place_ref, core_ref, all_factor_ref, factor_ref, q_ref, do_ref, e_ref, es_ref,
+    offset_ref, place_ref, all_factor_ref, factor_ref, q_ref, do_ref, e_ref, es_ref,
     at00, at01, at10, at11, bt00, bt01, bt10, bt11, term_ref, keep_ref, send_ref, row_scr,
 ):
     step = pl.program_id(0)
@@ -329,20 +323,20 @@
     rest = jnp.dot(es_ref[...], jnp.concatenate(narrow_rhs, axis=0), preferred_element_type=F32)
     grad_v = both[:, :HD]
     grad_k = (both[:, HD:] + rest) * SCALE
-    even_core = core_ref[0] == 0
+    even_core = place_ref[2] == 0
     pieces, size = keep_ref.shape[0], keep_ref.shape[1]
     for at, grad in ((0, grad_k), (HD, grad_v)):
         for piece in range(pieces):
             even = grad[2 * piece * size : (2 * piece + 1) * size]
             odd = grad[(2 * piece + 1) * size : (2 * piece + 2) * size]
             y, x = divmod(piece, pieces // 2)
-            x_offset = lax.rem(x + pieces // 2 - core_ref[2], pieces // 2)
-            slot = 2 * x_offset + lax.rem(core_ref[1] + y, 2)
+            x_offset = lax.rem(x + pieces // 2 - place_ref[4], pieces // 2)
+            slot = 2 * x_offset + lax.rem(place_ref[3] + y, 2)
             keep_ref[slot, :, at : at + HD] = jnp.where(even_core, even, odd)
             send_ref[slot, :, at : at + HD] = jnp.where(even_core, odd, even)
 
 
-def term_part(order, place, core, factors, queries, grad_out, e, es, at, bt, pieces):
+def term_part(order, place, factors, queries, grad_out, e, es, at, bt, pieces):
     rows, width = queries.shape
     image_rows, wide = e.shape
     heads = factors.shape[1]
@@ -354,7 +348,7 @@
     offsets = jnp.array(order + order[-2:], jnp.int32)
 
     def spec(i, slot):
-        def index(g, offset, place, core):
+        def index(g, offset, place):
             return 0, pair_at(place, offset[2 * g + i], slot, pairs)
 
         return pl.BlockSpec((HD, 2 * rows), index)
@@ -363,7 +357,7 @@
     half = jax.ShapeDtypeStruct((pieces, size, groups * 2 * HD), F32)
     half_spec = pl.BlockSpec((pieces, size, 2 * HD), lambda g, *_: (0, 0, g))
     grid_spec = pltpu.PrefetchScalarGridSpec(
-        num_scalar_prefetch=3,
+        num_scalar_prefetch=2,
         grid=(groups,),
         in_specs=[
             pl.BlockSpec((2, heads, rows), lambda g, *_: (0, 0, 0)),
@@ -387,7 +381,7 @@
             flops=6 * width * rows * image_rows, bytes_accessed=20 * 2**20, transcendentals=0
         ),
         name="query_and_image_terms",
-    )(offsets, place, core, factors, factors, queries, grad_out, e, es, *[at] * 4, *[bt] * 4)
+    )(offsets, place, factors, factors, queries, grad_out, e, es, *[at] * 4, *[bt] * 4)
 
 
 def on_device(queries, keys, values, grad_out, keep_blocks):
@@ -400,10 +394,17 @@
     swap_far = [(t, (t + pieces) % text_size) for t in range(text_size)]
     swap_core = [(t, t ^ 1) for t in range(text_size)]
     image_index = lax.axis_index("image").astype(jnp.int32)
-    place = jnp.stack([image_index // z_size, image_index % z_size])
     text_index = lax.axis_index("text").astype(jnp.int32)
     x_size = pieces // 2
-    core = jnp.stack([text_index % 2, text_index // pieces, text_index // 2 % x_size])
+    place = jnp.stack(
+        [
+            image_index // z_size,
+            image_index % z_size,
+            text_index % 2,
+            text_index // pieces,
+            text_index // 2 % x_size,
+        ]
+    )
 
     def turn_x(by):
         return [
@@ -429,7 +430,7 @@
     left = lax.ppermute(first_left, "image", turn(-1))
     order = piece_offsets(z_size)[2:]
     terms, keep, send = term_part(
-        order, place, core, factors, queries, grad_out, e, es, at, bt, pieces
+        order, place, factors, queries, grad_out, e, es, at, bt, pieces
     )
     terms, keep, send, right, left = lax.optimization_barrier((terms, keep, send, right, left))
     term = {offset: terms[i] for i, offset in enumerate(order)}

time: 89 us -> 88 us (0.989)
  other arithmetic: 4.28 us -> 3.03 us
    another operation x3 -> x1, other arithmetic: 1.27 us -> 0.02 us  [the longest x1 0.66 us: on_device(): place = jnp.stack([image_index // z_size, image_index % z_size])]
where the time goes in v4:
time: 88 us; the launch traced here: 87.6 us
  Pallas kernels  30.2 us (34%)
  starting transfers between devices  27 us (31%)
  waiting for transfers between devices  25 us (28%)
  other arithmetic  3.03 us (3%)
  local copies, waits for them, and re-layouts  1.59 us (2%)
    pallas_call x1, Pallas kernels, term_part(): pl.pallas_call(term_kernel, grid_spec=grid_spec, out_shape=[jax.ShapeDtyp...  10.5 us
    all_to_all x1, starting transfers between devices, on_device(): stats = lax.all_to_all(own, 'image', 0, 0, tiled=True)  9.96 us
    pallas_call x1, Pallas kernels, product_part(): pl.pallas_call(product_kernel, grid=(groups,), in_specs=[pl.BlockSpec((1,...  8.97 us
    pallas_call x1, Pallas kernels, local_part(): pl.pallas_call(local_kernel, grid=(groups,), in_specs=[pl.BlockSpec(memor...  7.57 us
    all_to_all x1, waiting for transfers between devices, on_device(): stats = lax.all_to_all(own, 'image', 0, 0, tiled=True)  4.82 us
    ppermute x1, waiting for transfers between devices, on_device(): left = lax.ppermute(left + term[-2], 'image', turn(-1))  3.44 us
    pallas_call x1, Pallas kernels, merge_part(): pl.pallas_call(merge_kernel, grid_spec=grid_spec, out_shape=[piece, piece...  3.16 us
    ppermute x1, waiting for transfers between devices, on_device(): right = lax.ppermute(right + term[2], 'image', turn(1))  3.09 us
  transfers between devices with their start and end apart: 16, of which 11 were waited for; matrix products, arithmetic and copies ran while one was open for 4% of the time, Pallas kernels for 22%

profile of v4, /device:TPU:8, one launch (start us, length us, event | category | flops | bytes accessed | tf_op | source)
XLA Modules:
  0.0 87.6 jit_solution(9482526173627275536)
XLA Ops:
  0.6 7.6 %local_statistics.1 = (bf16[640,4096]{1,0:T(8,128)(2,1)}, f32[16,64,128]{2,1,0:T(8,128)}, f32[32,128]{1,0:T(8,128)}) custom-call(s32[2,5]{1,0:T(2,128)} %keep_ref.1, bf16[128,4096]{1,0:T(8,128)(2,1)} %q_ref.3, bf16[128,4096]{1,0:T(8,128)(2,1)} %do_ref.5, bf16[640,512]{1,0:T(8,128)(2,1)} %k_ref.3, bf16[640,512]{1,0:T(8,128)(2,1)} %v_ref.3), custom_call_target="tpu_custom_call" | custom-call | flops 1342177280 | bytes 9437184 | tf_op jit(solution)/shard_map/local_statistics/pallas_call | solution.py:105
  8.2 10.0 %all-to-all-start = ((f32[16,64,128]{2,1,0:T(8,128)}), f32[16,64,128]{2,1,0:T(8,128)S(1)}, u32[]{:S(2)}, u32[]{:S(2)}) async-start(f32[16,64,128]{2,1,0:T(8,128)} %get-tuple-element.26.own_ref), calls=%async_computation | async-start | bytes 1048576 | tf_op jit(solution)/shard_map/all_to_all | solution.py:425
  18.8 9.0 %local_products.1 = (bf16[640,4096]{1,0:T(8,128)(2,1)}, f32[128,4096]{1,0:T(8,128)}, f32[128,4096]{1,0:T(8,128)}) custom-call(f32[16,64,128]{2,1,0:T(8,128)} %get-tuple-element.26.own_ref, bf16[128,4096]{1,0:T(8,128)(2,1)} %do_ref.5, bf16[640,512]{1,0:T(8,128)(2,1)} %k_ref.3, bf16[640,512]{1,0:T(8,128)(2,1)} %v_ref.3, bf16[640,4096]{1,0:T(8,128)(2,1)} %get-tuple-element.28.e_ref), custom_call_target="tpu_custom_call" | custom-call | flops 2013265920 | bytes 18874368 | tf_op jit(solution)/shard_map/local_products/pallas_call | solution.py:164
  27.8 4.8 %all-to-all-done.all_ref = f32[16,64,128]{2,1,0:T(8,128)S(1)} async-done(((f32[16,64,128]{2,1,0:T(8,128)}), f32[16,64,128]{2,1,0:T(8,128)S(1)}, u32[]{:S(2)}, u32[]{:S(2)}) %all-to-all-start) | async-done | bytes 524320 | tf_op jit(solution)/shard_map/all_to_all | solution.py:425
  33.4 3.2 %merged_statistics.1 = (f32[2,128,256]{2,1,0:T(8,128)}, f32[2,128,256]{2,1,0:T(8,128)}, f32[2,32,128]{2,1,0:T(8,128)}) custom-call(s32[5]{0:T(128)} %stack.35.place_ref, f32[16,64,128]{2,1,0:T(8,128)} %copy-done, f32[16,64,128]{2,1,0:T(8,128)} %get-tuple-element.26.own_ref, f32[32,128]{1,0:T(8,128)} %get-tuple-element.27.max_ref, ...), custom_call_target="tpu_custom_call" | custom-call | flops 524288 | bytes 3145728 | tf_op jit(solution)/shard_map/merged_statistics/pallas_call | solution.py:278
  36.6 2.1 %collective-permute-start = (f32[2,128,256]{2,1,0:T(8,128)}, f32[2,128,256]{2,1,0:T(8,128)S(1)}, u32[]{:S(2)}, u32[]{:S(2)}) collective-permute-start(f32[2,128,256]{2,1,0:T(8,128)} %get-tuple-element.36), channel_id=1, source_target_pairs={{0,1},{1,2},{2,3},{3,4},{4,5},{5,6},{6,7},{7,0},{8,9},{9,10},{10,1... | collective-permute-start | bytes 786440 | tf_op jit(solution)/shard_map/ppermute | solution.py:429
  39.8 10.5 %query_and_image_terms.1 = (f32[8,2,128,256]{3,2,1,0:T(8,128)}, f32[8,40,1024]{2,1,0:T(8,128)}, f32[8,40,1024]{2,1,0:T(8,128)}) custom-call(s32[8]{0:T(128)} %constant.68.clone.offset_ref, s32[5]{0:T(128)} %stack.35.place_ref, f32[2,32,128]{2,1,0:T(8,128)} %get-tuple-element.31.all_factor_ref.factor_ref, ...), custom_call_target="tpu_custom_call" | custom-call | flops 2013265920 | bytes 20971520 | tf_op jit(solution)/shard_map/query_and_image_terms/pallas_call | solution.py:375
  50.5 1.2 %bitcast_add_fusion.4 = (f32[2,128,256]{2,1,0:T(8,128)S(1)}, f32[2,128,256]{2,1,0:T(8,128)S(1)}) fusion(f32[2,128,256]{2,1,0:T(8,128)S(1)} %collective-permute-done.1, f32[8,2,128,256]{3,2,1,0:T(8,128)} %get-tuple-element.39, f32[2,128,256]{2,1,0:T(8,128)S(1)} %collective-permute-done), kind=kLoop, calls=%fused_computation.8 | loop fusion | flops 131072 | bytes 1572864 | tf_op jit(solution)/shard_map/add | solution.py:439
  51.7 1.5 %collective-permute-start.3 = (f32[2,128,256]{2,1,0:T(8,128)S(1)}, f32[2,128,256]{2,1,0:T(8,128)S(1)}, u32[]{:S(2)}, u32[]{:S(2)}) collective-permute-start(f32[2,128,256]{2,1,0:T(8,128)S(1)} %get-tuple-element.53), channel_id=1, source_target_pairs={{0,7},{1,0},{2,1},{3,2},{4,3},{5,4},{6,5},{7,6},{8,15},{9,8},{10,9... | collective-permute-start | bytes 786440 | tf_op jit(solution)/shard_map/ppermute | solution.py:439
  54.1 2.8 %collective-permute-start.6 = (f32[40,1024]{1,0:T(8,128)S(1)}, f32[40,1024]{1,0:T(8,128)S(1)}, u32[]{:S(2)}, u32[]{:S(2)}) collective-permute-start(f32[40,1024]{1,0:T(8,128)S(1)} %get-tuple-element.59), channel_id=1, source_target_pairs={{0,96},{16,112},{32,0},{48,16},{64,32},{80,48},{96,64},{112,80},{1... | collective-permute-start | bytes 491528 | tf_op jit(solution)/shard_map/ppermute | solution.py:443
  56.9 3.4 %collective-permute-done.3 = f32[2,128,256]{2,1,0:T(8,128)S(1)} collective-permute-done((f32[2,128,256]{2,1,0:T(8,128)S(1)}, f32[2,128,256]{2,1,0:T(8,128)S(1)}, u32[]{:S(2)}, u32[]{:S(2)}) %collective-permute-start.3) | collective-permute-done | bytes 262176 | tf_op jit(solution)/shard_map/ppermute | solution.py:439
  60.4 2.3 %collective-permute-done.2 = f32[2,128,256]{2,1,0:T(8,128)S(1)} collective-permute-done((f32[2,128,256]{2,1,0:T(8,128)S(1)}, f32[2,128,256]{2,1,0:T(8,128)S(1)}, u32[]{:S(2)}, u32[]{:S(2)}) %collective-permute-start.2) | collective-permute-done | bytes 262176 | tf_op jit(solution)/shard_map/ppermute | solution.py:438
  62.7 1.3 %collective-permute-done.5 = f32[40,1024]{1,0:T(8,128)S(1)} collective-permute-done((f32[40,1024]{1,0:T(8,128)S(1)}, f32[40,1024]{1,0:T(8,128)S(1)}, u32[]{:S(2)}, u32[]{:S(2)}) %collective-permute-start.5) | collective-permute-done | bytes 163872 | tf_op jit(solution)/shard_map/ppermute | solution.py:442
  64.1 2.5 %collective-permute-start.8 = (f32[2,128,256]{2,1,0:T(8,128)S(1)}, f32[2,128,256]{2,1,0:T(8,128)S(1)}, u32[]{:S(2)}, u32[]{:S(2)}) collective-permute-start(f32[2,128,256]{2,1,0:T(8,128)S(1)} %get-tuple-element.51), channel_id=1, source_target_pairs={{0,7},{1,0},{2,1},{3,2},{4,3},{5,4},{6,5},{7,6},{8,15},{9,8},{10,9... | collective-permute-start | bytes 786440 | tf_op jit(solution)/shard_map/ppermute | solution.py:446
  66.7 1.1 %collective-permute-start.13 = (f32[2,40,1024]{2,1,0:T(8,128)S(1)}, f32[2,40,1024]{2,1,0:T(8,128)S(1)}, u32[]{:S(2)}, u32[]{:S(2)}) collective-permute-start(f32[2,40,1024]{2,1,0:T(8,128)S(1)} %pad_maximum_fusion.1), channel_id=1, source_target_pairs={{0,96},{16,112},{32,0},{48,16},{64,32},{80,48},{96,64},{112,80},{1... | collective-permute-start | bytes 983048 | tf_op jit(solution)/shard_map/ppermute | solution.py:448
  67.8 1.2 %collective-permute-start.12 = (f32[2,40,1024]{2,1,0:T(8,128)S(1)}, f32[2,40,1024]{2,1,0:T(8,128)S(1)}, u32[]{:S(2)}, u32[]{:S(2)}) collective-permute-start(f32[2,40,1024]{2,1,0:T(8,128)S(1)} %pad_maximum_fusion), channel_id=1, source_target_pairs={{0,32},{16,48},{32,64},{48,80},{64,96},{80,112},{96,0},{112,16},{1... | collective-permute-start | bytes 983048 | tf_op jit(solution)/shard_map/ppermute | solution.py:447
  69.1 2.3 %collective-permute-done.8 = f32[2,128,256]{2,1,0:T(8,128)S(1)} collective-permute-done((f32[2,128,256]{2,1,0:T(8,128)S(1)}, f32[2,128,256]{2,1,0:T(8,128)S(1)}, u32[]{:S(2)}, u32[]{:S(2)}) %collective-permute-start.8) | collective-permute-done | bytes 262176 | tf_op jit(solution)/shard_map/ppermute | solution.py:446
  71.3 3.1 %collective-permute-done.7 = f32[2,128,256]{2,1,0:T(8,128)S(1)} collective-permute-done((f32[2,128,256]{2,1,0:T(8,128)S(1)}, f32[2,128,256]{2,1,0:T(8,128)S(1)}, u32[]{:S(2)}, u32[]{:S(2)}) %collective-permute-start.7) | collective-permute-done | bytes 262176 | tf_op jit(solution)/shard_map/ppermute | solution.py:445
  74.5 1.4 %collective-permute-start.11 = (f32[128,256]{1,0:T(8,128)S(1)}, f32[128,256]{1,0:T(8,128)S(1)}, u32[]{:S(2)}, u32[]{:S(2)}) collective-permute-start(f32[128,256]{1,0:T(8,128)S(1)} %slice_bitcast_fusion.6), channel_id=1, source_target_pairs={{0,8},{1,9},{2,10},{3,11},{4,12},{5,13},{6,14},{7,15},{8,0},{9,1},... | collective-permute-start | bytes 393224 | tf_op jit(solution)/shard_map/ppermute | solution.py:458
  76.1 1.3 %collective-permute-done.12 = f32[2,40,1024]{2,1,0:T(8,128)S(1)} collective-permute-done((f32[2,40,1024]{2,1,0:T(8,128)S(1)}, f32[2,40,1024]{2,1,0:T(8,128)S(1)}, u32[]{:S(2)}, u32[]{:S(2)}) %collective-permute-start.12) | collective-permute-done | bytes 327712 | tf_op jit(solution)/shard_map/ppermute | solution.py:447
  77.5 2.4 %collective-permute-start.14 = (f32[40,1024]{1,0:T(8,128)S(1)}, f32[40,1024]{1,0:T(8,128)S(1)}, u32[]{:S(2)}, u32[]{:S(2)}) collective-permute-start(f32[40,1024]{1,0:T(8,128)S(1)} %slice_bitcast_fusion), channel_id=1, source_target_pairs={{0,128},{16,144},{32,160},{48,176},{64,192},{80,208},{96,224},{112... | collective-permute-start | bytes 491528 | tf_op jit(solution)/shard_map/ppermute | solution.py:451
  79.9 1.9 %collective-permute-done.11 = f32[128,256]{1,0:T(8,128)S(1)} collective-permute-done((f32[128,256]{1,0:T(8,128)S(1)}, f32[128,256]{1,0:T(8,128)S(1)}, u32[]{:S(2)}, u32[]{:S(2)}) %collective-permute-start.11) | collective-permute-done | bytes 131104 | tf_op jit(solution)/shard_map/ppermute | solution.py:458
  82.2 1.7 %collective-permute-done.10 = f32[128,256]{1,0:T(8,128)S(1)} collective-permute-done((f32[128,256]{1,0:T(8,128)S(1)}, f32[128,256]{1,0:T(8,128)S(1)}, u32[]{:S(2)}, u32[]{:S(2)}) %collective-permute-start.10) | collective-permute-done | bytes 131104 | tf_op jit(solution)/shard_map/ppermute | solution.py:457
  84.5 2.4 %collective-permute-done.14 = f32[40,1024]{1,0:T(8,128)S(1)} collective-permute-done((f32[40,1024]{1,0:T(8,128)S(1)}, f32[40,1024]{1,0:T(8,128)S(1)}, u32[]{:S(2)}, u32[]{:S(2)}) %collective-permute-start.14) | collective-permute-done | bytes 163872 | tf_op jit(solution)/shard_map/ppermute | solution.py:451
  (35 shorter events, 5.8 us)
Async XLA Ops:
  8.2 24.4 %all-to-all-start = ((f32[16,64,128]{2,1,0:T(8,128)}), f32[16,64,128]{2,1,0:T(8,128)S(1)}, u32[]{:S(2)}, u32[]{:S(2)}) async-start(f32[16,64,128]{2,1,0:T(8,128)} %get-tuple-element.26.own_ref), calls=%async_computation | async-start | bytes 1048576 | tf_op jit(solution)/shard_map/all_to_all | solution.py:425
  32.6 0.8 copy-start
  36.6 13.8 %collective-permute-start = (f32[2,128,256]{2,1,0:T(8,128)}, f32[2,128,256]{2,1,0:T(8,128)S(1)}, u32[]{:S(2)}, u32[]{:S(2)}) collective-permute-start(f32[2,128,256]{2,1,0:T(8,128)} %get-tuple-element.36), channel_id=1, source_target_pairs={{0,1},{1,2},{2,3},{3,4},{4,5},{5,6},{6,7},{7,0},{8,9},{9,10},{10,1... | collective-permute-start | bytes 786440 | tf_op jit(solution)/shard_map/ppermute | solution.py:429
  38.7 11.7 %collective-permute-start.1 = (f32[2,128,256]{2,1,0:T(8,128)}, f32[2,128,256]{2,1,0:T(8,128)S(1)}, u32[]{:S(2)}, u32[]{:S(2)}) collective-permute-start(f32[2,128,256]{2,1,0:T(8,128)} %get-tuple-element.37), channel_id=1, source_target_pairs={{0,7},{1,0},{2,1},{3,2},{4,3},{5,4},{6,5},{7,6},{8,15},{9,8},{10,9... | collective-permute-start | bytes 786440 | tf_op jit(solution)/shard_map/ppermute | solution.py:430
  50.4 3.4 %copy-start.1 = (f32[8,40,1024]{2,1,0:T(8,128)S(1)}, f32[8,40,1024]{2,1,0:T(8,128)}, u32[]{:S(2)}) copy-start(f32[8,40,1024]{2,1,0:T(8,128)} %get-tuple-element.41) | copy-start | bytes 3932164
  50.4 3.4 %collective-permute-start.4 = (f32[8,40,1024]{2,1,0:T(8,128)}, f32[8,40,1024]{2,1,0:T(8,128)S(1)}, u32[]{:S(2)}, u32[]{:S(2)}) collective-permute-start(f32[8,40,1024]{2,1,0:T(8,128)} %get-tuple-element.42), channel_id=1, source_target_pairs={{0,16},{16,0},{32,48},{48,32},{64,80},{80,64},{96,112},{112,96},{1... | collective-permute-start | bytes 3932168 | tf_op jit(solution)/shard_map/ppermute | solution.py:437
  51.7 8.7 %collective-permute-start.3 = (f32[2,128,256]{2,1,0:T(8,128)S(1)}, f32[2,128,256]{2,1,0:T(8,128)S(1)}, u32[]{:S(2)}, u32[]{:S(2)}) collective-permute-start(f32[2,128,256]{2,1,0:T(8,128)S(1)} %get-tuple-element.53), channel_id=1, source_target_pairs={{0,7},{1,0},{2,1},{3,2},{4,3},{5,4},{6,5},{7,6},{8,15},{9,8},{10,9... | collective-permute-start | bytes 786440 | tf_op jit(solution)/shard_map/ppermute | solution.py:439
  53.1 10.9 %copy-start.2 = (f32[8,2,128,256]{3,2,1,0:T(8,128)S(1)}, f32[8,2,128,256]{3,2,1,0:T(8,128)}, u32[]{:S(2)}) copy-start(f32[8,2,128,256]{3,2,1,0:T(8,128)} %get-tuple-element.39) | copy-start | bytes 6291460
  53.1 9.6 %collective-permute-start.2 = (f32[2,128,256]{2,1,0:T(8,128)S(1)}, f32[2,128,256]{2,1,0:T(8,128)S(1)}, u32[]{:S(2)}, u32[]{:S(2)}) collective-permute-start(f32[2,128,256]{2,1,0:T(8,128)S(1)} %get-tuple-element.54), channel_id=1, source_target_pairs={{0,1},{1,2},{2,3},{3,4},{4,5},{5,6},{6,7},{7,0},{8,9},{9,10},{10,1... | collective-permute-start | bytes 786440 | tf_op jit(solution)/shard_map/ppermute | solution.py:438
  54.1 8.6 %collective-permute-start.6 = (f32[40,1024]{1,0:T(8,128)S(1)}, f32[40,1024]{1,0:T(8,128)S(1)}, u32[]{:S(2)}, u32[]{:S(2)}) collective-permute-start(f32[40,1024]{1,0:T(8,128)S(1)} %get-tuple-element.59), channel_id=1, source_target_pairs={{0,96},{16,112},{32,0},{48,16},{64,32},{80,48},{96,64},{112,80},{1... | collective-permute-start | bytes 491528 | tf_op jit(solution)/shard_map/ppermute | solution.py:443
  56.9 7.1 %collective-permute-start.5 = (f32[40,1024]{1,0:T(8,128)S(1)}, f32[40,1024]{1,0:T(8,128)S(1)}, u32[]{:S(2)}, u32[]{:S(2)}) collective-permute-start(f32[40,1024]{1,0:T(8,128)S(1)} %get-tuple-element.60), channel_id=1, source_target_pairs={{0,32},{16,48},{32,64},{48,80},{64,96},{80,112},{96,0},{112,16},{1... | collective-permute-start | bytes 491528 | tf_op jit(solution)/shard_map/ppermute | solution.py:442
  64.1 7.2 %collective-permute-start.8 = (f32[2,128,256]{2,1,0:T(8,128)S(1)}, f32[2,128,256]{2,1,0:T(8,128)S(1)}, u32[]{:S(2)}, u32[]{:S(2)}) collective-permute-start(f32[2,128,256]{2,1,0:T(8,128)S(1)} %get-tuple-element.51), channel_id=1, source_target_pairs={{0,7},{1,0},{2,1},{3,2},{4,3},{5,4},{6,5},{7,6},{8,15},{9,8},{10,9... | collective-permute-start | bytes 786440 | tf_op jit(solution)/shard_map/ppermute | solution.py:446
  66.6 7.8 %collective-permute-start.7 = (f32[2,128,256]{2,1,0:T(8,128)S(1)}, f32[2,128,256]{2,1,0:T(8,128)S(1)}, u32[]{:S(2)}, u32[]{:S(2)}) collective-permute-start(f32[2,128,256]{2,1,0:T(8,128)S(1)} %get-tuple-element.52), channel_id=1, source_target_pairs={{0,1},{1,2},{2,3},{3,4},{4,5},{5,6},{6,7},{7,0},{8,9},{9,10},{10,1... | collective-permute-start | bytes 786440 | tf_op jit(solution)/shard_map/ppermute | solution.py:445
  66.7 9.4 %collective-permute-start.13 = (f32[2,40,1024]{2,1,0:T(8,128)S(1)}, f32[2,40,1024]{2,1,0:T(8,128)S(1)}, u32[]{:S(2)}, u32[]{:S(2)}) collective-permute-start(f32[2,40,1024]{2,1,0:T(8,128)S(1)} %pad_maximum_fusion.1), channel_id=1, source_target_pairs={{0,96},{16,112},{32,0},{48,16},{64,32},{80,48},{96,64},{112,80},{1... | collective-permute-start | bytes 983048 | tf_op jit(solution)/shard_map/ppermute | solution.py:448
  67.8 9.6 %collective-permute-start.12 = (f32[2,40,1024]{2,1,0:T(8,128)S(1)}, f32[2,40,1024]{2,1,0:T(8,128)S(1)}, u32[]{:S(2)}, u32[]{:S(2)}) collective-permute-start(f32[2,40,1024]{2,1,0:T(8,128)S(1)} %pad_maximum_fusion), channel_id=1, source_target_pairs={{0,32},{16,48},{32,64},{48,80},{64,96},{80,112},{96,0},{112,16},{1... | collective-permute-start | bytes 983048 | tf_op jit(solution)/shard_map/ppermute | solution.py:447
  74.5 7.3 %collective-permute-start.11 = (f32[128,256]{1,0:T(8,128)S(1)}, f32[128,256]{1,0:T(8,128)S(1)}, u32[]{:S(2)}, u32[]{:S(2)}) collective-permute-start(f32[128,256]{1,0:T(8,128)S(1)} %slice_bitcast_fusion.6), channel_id=1, source_target_pairs={{0,8},{1,9},{2,10},{3,11},{4,12},{5,13},{6,14},{7,15},{8,0},{9,1},... | collective-permute-start | bytes 393224 | tf_op jit(solution)/shard_map/ppermute | solution.py:458
  75.9 6.3 %collective-permute-start.9 = (f32[128,256]{1,0:T(8,128)S(1)}, f32[128,256]{1,0:T(8,128)S(1)}, u32[]{:S(2)}, u32[]{:S(2)}) collective-permute-start(f32[128,256]{1,0:T(8,128)S(1)} %get-tuple-element.61), channel_id=1, source_target_pairs={{0,1},{1,2},{2,3},{3,4},{4,5},{5,6},{6,7},{7,0},{8,9},{9,10},{10,1... | collective-permute-start | bytes 393224 | tf_op jit(solution)/shard_map/ppermute | solution.py:456
  76.0 7.8 %collective-permute-start.10 = (f32[128,256]{1,0:T(8,128)S(1)}, f32[128,256]{1,0:T(8,128)S(1)}, u32[]{:S(2)}, u32[]{:S(2)}) collective-permute-start(f32[128,256]{1,0:T(8,128)S(1)} %get-tuple-element.62), channel_id=1, source_target_pairs={{0,9},{1,10},{2,11},{3,12},{4,13},{5,14},{6,15},{7,8},{8,1},{9,2},... | collective-permute-start | bytes 393224 | tf_op jit(solution)/shard_map/ppermute | solution.py:457
  77.5 9.5 %collective-permute-start.14 = (f32[40,1024]{1,0:T(8,128)S(1)}, f32[40,1024]{1,0:T(8,128)S(1)}, u32[]{:S(2)}, u32[]{:S(2)}) collective-permute-start(f32[40,1024]{1,0:T(8,128)S(1)} %slice_bitcast_fusion), channel_id=1, source_target_pairs={{0,128},{16,144},{32,160},{48,176},{64,192},{80,208},{96,224},{112... | collective-permute-start | bytes 491528 | tf_op jit(solution)/shard_map/ppermute | solution.py:451
